TPU v7x, 512 devices: a whole 4x4x16 slice. The times are simulated.
512 devices in a mesh: lat: 8 (over x_lo, y), lon: 64 (over x_hi, z, core).
Axes of the slice: x: 4 (x_hi: 2, x_lo: 2; x = x_hi * 2 + x_lo), y: 4, z: 16, core: 2. Of those that a mesh axis runs over, the one named last changes fastest.
Arguments:
- signal: bfloat16 [384, 512, 256], P('lat', 'lon'), may hold values from -6 to 6
- cotangent: bfloat16 [384, 512, 256], P('lat', 'lon'), may hold values from -6 to 6
- weights: bfloat16 [4, 256, 256], replicated, may hold values from -0.1875 to 0.1875
- band_kernel: bfloat16 [4, 384, 3, 17], replicated, may hold values from -1.25 to 1.25
- cycle_kernel: bfloat16 [4, 4, 3, 512], replicated, may hold values from -0.15625 to 0.15625
- support_width: int32 [384], replicated, may hold values from 1 to 8, as said below
Outputs:
- conv_output: bfloat16 [384, 512, 256], P('lat', 'lon')
- signal_grad: bfloat16 [384, 512, 256], P('lat', 'lon')
- weight_grad: float32 [4, 256, 256], replicated
Inputs may be any that keep to these rules, and one draw needn't show every extreme that they name: `support_width`: some row has the half-width 8.
All inputs are finite; a program needn't handle non-finite values.
Results may differ from a plain program's by a relative error of at most 0.0049.
Values may be sent and summed in bfloat16 or wider, within the bound.
A program may use at most 64 MiB of HBM per device.

v0:
```python
import math

import jax
import jax.numpy as jnp
from jax import lax
from jax.sharding import PartitionSpec as P

K = 4
R = 1
H = 8
P_SIZE = 2


precise = lax.Precision.HIGHEST


def with_halo(x, sides, width, wrap):
    for axis, dim in sides:
        devices, length = (lax.axis_size(axis), x.shape[dim])
        up = [(i, (i + 1) % devices) for i in range(devices if wrap else devices - 1)]
        down = [(j, i) for i, j in up]
        last = lax.slice_in_dim(x, length - width, length, axis=dim)
        first = lax.slice_in_dim(x, 0, width, axis=dim)
        before = lax.ppermute(last, axis, up)
        after = lax.ppermute(first, axis, down)
        x = jnp.concatenate([before, x, after], axis=dim)
    return x


def lag_table(lon_count, forward):
    outputs = jnp.arange(lon_count, dtype=jnp.int32)[:, None, None]
    inputs = jnp.arange(lon_count + 2 * H, dtype=jnp.int32)[None, :, None]
    shifts = jnp.arange(2 * H + 1, dtype=jnp.int32)[None, None, :]
    if forward:
        matched = outputs - inputs + 2 * H == shifts
    else:
        matched = inputs - outputs == shifts
    return matched.astype(jnp.float32)


def local_coefficients(band_kernel, support_width, first_row, total_rows, row_count):
    padded_kernel = jnp.pad(band_kernel, ((0, 0), (R, R), (0, 0), (0, 0)))
    padded_width = jnp.pad(support_width, (R, R))
    kernel_rows = lax.dynamic_slice_in_dim(padded_kernel, first_row, row_count, 1).astype(
        jnp.float32
    )
    width_rows = lax.dynamic_slice_in_dim(padded_width, first_row, row_count, 0)
    global_rows = first_row - R + jnp.arange(row_count, dtype=jnp.int32)
    polar_rows = (global_rows < P_SIZE) | (global_rows >= total_rows - P_SIZE)
    offsets = jnp.abs(jnp.arange(2 * H + 1, dtype=jnp.int32) - H)
    allowed = (offsets[None, :] <= width_rows[:, None]) & jnp.logical_not(polar_rows)[:, None]
    return kernel_rows * allowed[None, :, None, :].astype(jnp.float32)


def local(signal, cotangent, weights, band_kernel, cycle_kernel, support_width):
    lat_count, lon_count, channels = signal.shape
    lat_index = lax.axis_index("lat")
    lon_index = lax.axis_index("lon")
    lat_devices = lax.axis_size("lat")
    lon_total = lon_count * lax.axis_size("lon")
    total_rows = lat_count * lat_devices
    first_row = lat_index * lat_count
    is_top = lat_index == 0
    is_polar = is_top | (lat_index == lat_devices - 1)
    coeffs = local_coefficients(
        band_kernel, support_width, first_row, total_rows, lat_count + 2 * R
    )
    forward_mats = jnp.einsum(
        "ktrd,amd->ktram",
        coeffs[:, R : R + lat_count],
        lag_table(lon_count, True),
        precision=precise,
    ).astype(jnp.bfloat16)
    backward_mats = jnp.einsum(
        "ktrd,amd->ktram", coeffs, lag_table(lon_count, False), precision=precise
    ).astype(jnp.bfloat16)
    pole_kernel = lax.dynamic_slice_in_dim(cycle_kernel, jnp.where(is_top, 0, P_SIZE), P_SIZE, 1)
    out_lons = lon_index * lon_count + jnp.arange(lon_count, dtype=jnp.int32)
    cycle_lons = jnp.arange(lon_total, dtype=jnp.int32)
    stacked = jnp.stack([signal, cotangent])
    rows_both = with_halo(stacked, (("lat", 1),), R, False)
    signal_slab = jnp.where(is_top, signal[: P_SIZE + R], signal[lat_count - P_SIZE - R :])
    ext_signal = with_halo(rows_both[0], (("lon", 1),), H, True)
    cycle_signal = lax.all_gather(signal_slab, "lon", axis=1, tiled=True)
    filtered = jnp.zeros((K, lat_count, lon_count, channels), jnp.float32)
    for lat_tap in range(2 * R + 1):
        filtered = filtered + jnp.einsum(
            "kiam,imc->kiac",
            forward_mats[:, :, lat_tap],
            ext_signal[lat_tap : lat_tap + lat_count],
            preferred_element_type=jnp.float32,
        )
    zero_rows = jnp.zeros((R,) + cycle_signal.shape[1:], cycle_signal.dtype)
    cycle_padded = jnp.where(
        is_top,
        jnp.concatenate([zero_rows, cycle_signal]),
        jnp.concatenate([cycle_signal, zero_rows]),
    )

    def polar_forward():
        circulant = pole_kernel[:, :, :, (out_lons[:, None] - cycle_lons[None, :]) % lon_total]
        result = jnp.zeros((K, P_SIZE, lon_count, channels), jnp.float32)
        for lat_tap in range(2 * R + 1):
            result = result + jnp.einsum(
                "kpam,pmc->kpac",
                circulant[:, :, lat_tap],
                cycle_padded[lat_tap : lat_tap + P_SIZE],
                preferred_element_type=jnp.float32,
            )
        return result

    def forward_skip():
        return jnp.zeros((K, P_SIZE, lon_count, channels), jnp.float32)

    polar_part = lax.cond(is_polar, polar_forward, forward_skip)
    remain = lat_count - P_SIZE
    filtered = filtered + jnp.where(
        is_top,
        jnp.pad(polar_part, ((0, 0), (0, remain), (0, 0), (0, 0))),
        jnp.pad(polar_part, ((0, 0), (remain, 0), (0, 0), (0, 0))),
    )
    filtered = filtered.astype(jnp.bfloat16)
    conv_output = jnp.einsum(
        "kiac,kce->iae", filtered, weights, preferred_element_type=jnp.float32
    ).astype(jnp.bfloat16)
    local_grad = jnp.einsum(
        "kiac,iae->kce", filtered, cotangent, preferred_element_type=jnp.float32
    )
    weight_grad = lax.psum(local_grad, ("lat", "lon")) * (1.0 / math.sqrt(total_rows * lon_total))
    mixed_rows = jnp.einsum(
        "tae,kce->ktac", rows_both[1], weights, preferred_element_type=jnp.float32
    ).astype(jnp.bfloat16)
    ext_grad = with_halo(mixed_rows, (("lon", 2),), H, True)
    mixed_slab = jnp.where(
        is_top, mixed_rows[:, R : R + P_SIZE], mixed_rows[:, R + lat_count - P_SIZE : R + lat_count]
    )
    cycle_mixed = lax.all_gather(mixed_slab, "lon", axis=2, tiled=True)
    signal_grad = jnp.zeros((lat_count, lon_count, channels), jnp.float32)
    for lat_tap in range(2 * R + 1):
        start = 2 * R - lat_tap
        signal_grad = signal_grad + jnp.einsum(
            "kjam,kjmc->jac",
            backward_mats[:, start : start + lat_count, lat_tap],
            ext_grad[:, start : start + lat_count],
            preferred_element_type=jnp.float32,
        )

    def polar_backward():
        circulant = pole_kernel[:, :, :, (cycle_lons[None, :] - out_lons[:, None]) % lon_total]
        result = jnp.zeros((P_SIZE + 2 * R, lon_count, channels), jnp.float32)
        for lat_tap in range(2 * R + 1):
            portion = jnp.einsum(
                "kpam,kpmc->pac",
                circulant[:, :, lat_tap],
                cycle_mixed,
                preferred_element_type=jnp.float32,
            )
            result = result + jnp.pad(portion, ((lat_tap, 2 * R - lat_tap), (0, 0), (0, 0)))
        return result

    def backward_skip():
        return jnp.zeros((P_SIZE + 2 * R, lon_count, channels), jnp.float32)

    polar_grad = lax.cond(is_polar, polar_backward, backward_skip)
    leftover = lat_count - P_SIZE - R
    signal_grad = signal_grad + jnp.where(
        is_top,
        jnp.pad(polar_grad[R:], ((0, leftover), (0, 0), (0, 0))),
        jnp.pad(polar_grad[: P_SIZE + R], ((leftover, 0), (0, 0), (0, 0))),
    )
    return (conv_output, signal_grad.astype(jnp.bfloat16), weight_grad)


def solution(mesh):
    placed = (P("lat", "lon", None), P("lat", "lon", None), P(), P(), P(), P())
    return jax.shard_map(
        local,
        mesh=mesh,
        in_specs=placed,
        out_specs=(P("lat", "lon", None), P("lat", "lon", None), P()),
        check_vma=False,
    )
```

profile of v0, /device:TPU:1, one launch (start us, length us, event | category | flops | bytes accessed | tf_op | source)
XLA Modules:
  0.0 708.2 jit_solution(16885316660159728370)
XLA Ops:
  8.8 4.0 collective-permute-start
  12.9 1.3 collective-permute-start.1
  15.9 86.1 %all_gather.6 = bf16[3,512,256]{2,1,0:T(8,128)(2,1)S(1)} all-gather(bf16[3,8,256]{2,1,0:T(8,128)(2,1)S(1)} %slice_select_fusion.1), channel_id=1, replica_groups=mesh['lat'=8,'lon'=64] {'lon'}, dimensions={1}, use_global_device_ids=true | all-gather | bytes 798720 | tf_op jit(solution)/shard_map/all_gather | solution.py:84
  103.8 1.3 copy.26
  105.2 1.3 copy.25
  106.5 1.3 copy.24
  108.6 2.1 collective-permute-start.3
  110.7 3.5 collective-permute-start.2
  114.2 1.9 copy.57
  116.1 51.4 %conditional.2 = (f32[4,48,8,256]{3,2,0,1:T(8,128)S(1)}, f32[4,48,8,256]{3,2,0,1:T(8,128)S(1)}) conditional(s32[]{:T(128)} %convert_element_type.57, () %tuple.39, (s32[8]{0:T(128)S(1)}, s32[512]{0:T(512)S(1)}, bf16[4,2,3,512]{0,1,3,2:T(2,128)(2,1)}, pred[]{:T(512)}, bf16[3,512,256]{2,1,0:T(8,128)(2,1)S(1)}) %tuple.40), branch_computations={%region_0.1_spmd, %region_1.2_spmd} | conditional | flops 50954240 | bytes 8030257 | solution.py:115
  116.3 41.3 %gather_fusion = bf16[4096,4,2,3]{1,2,3,0:T(2,128)(2,1)} fusion(bf16[4,2,3,512]{0,1,3,2:T(2,128)(2,1)} %get-tuple-element.70, s32[4096]{0:T(1024)S(1)} %broadcast_clamp_fusion), kind=kCustom, calls=%fused_computation | custom fusion | bytes 409600 | tf_op jit(solution)/shard_map/cond/branch_1_fun/gather | solution.py:101
  157.6 9.0 %copy.53 = bf16[8,512,4,2,3]{1,0,2,3,4:T(8,128)(2,1)S(1)} copy(bf16[8,512,4,2,3]{2,3,4,1,0:T(2,128)(2,1)} %bitcast.164) | data formatting | bytes 393216 | tf_op jit(solution)/shard_map/cond/branch_1_fun/gather | solution.py:101
  167.5 1.8 pad_maximum_fusion.1
  169.3 1.4 fusion.37
  171.1 1.9 fusion.12
  173.0 1.5 convolution_bitcast_fusion.3
  175.7 1.9 collective-permute-start.5
  177.6 3.8 collective-permute-start.4
  182.4 1.3 copy.28
  183.7 1.3 copy.30
  185.0 1.3 copy.29
  187.4 446.8 %all-reduce.17.cloned.1.call-done = f32[4,256,256]{2,1,0:T(8,128)} async-done(((f32[4,256,256]{2,1,0:T(8,128)}), f32[4,256,256]{2,1,0:T(8,128)}) %all-reduce.17.cloned.1.call-update) | async-done | bytes 1048592 | tf_op jit(solution)/shard_map/psum | solution.py:129
  634.2 2.4 broadcast_multiply_fusion
  636.6 1.6 pad_maximum_fusion
  639.2 1.4 fusion.17
  640.6 57.6 %conditional.3 = (f32[48,8,256]{2,1,0:T(8,128)}, f32[48,8,256]{2,1,0:T(8,128)}) conditional(s32[]{:T(128)} %convert_element_type.57, () %tuple.41, (s32[512]{0:T(512)S(1)}, s32[8]{0:T(128)S(1)}, bf16[4,2,3,512]{0,1,3,2:T(2,128)(2,1)}, bf16[4,2,512,256]{3,2,0,1:T(8,128)(2,1)}) %tuple.42), branch_computations={%region_2.3_spmd, %region_3.4_spmd} | conditional | flops 50413568 | bytes 16828500 | solution.py:164
  640.7 41.3 %gather_fusion.1 = bf16[4096,4,2,3]{1,2,3,0:T(2,128)(2,1)} fusion(bf16[4,2,3,512]{0,1,3,2:T(2,128)(2,1)} %get-tuple-element.75, s32[4096]{0:T(1024)S(1)} %broadcast_clamp_fusion.1), kind=kCustom, calls=%fused_computation.1 | custom fusion | bytes 409600 | tf_op jit(solution)/shard_map/cond/branch_1_fun/gather | solution.py:149
  682.0 9.9 %copy.54 = bf16[8,512,4,2,3]{1,0,2,3,4:T(8,128)(2,1)} copy(bf16[8,512,4,2,3]{2,3,4,1,0:T(2,128)(2,1)} %bitcast.165) | data formatting | bytes 393216 | tf_op jit(solution)/shard_map/cond/branch_1_fun/gather | solution.py:149
  691.9 2.1 convolution_bitcast_fusion.1
  694.1 1.2 convolution_bitcast_fusion.2
  695.4 1.2 convolution_bitcast_fusion
  698.2 2.6 fusion.32
  (77 shorter events, 12.4 us)
Async XLA Ops:
  8.0 166.6 %copy-start = (bf16[4,256,256]{2,1,0:T(8,128)(2,1)S(1)}, bf16[4,256,256]{2,1,0:T(8,128)(2,1)}, u32[]{:S(2)}) copy-start(bf16[4,256,256]{2,1,0:T(8,128)(2,1)} %param.12) | copy-start | bytes 1572868
  8.0 626.1 %all-reduce.17.cloned.1.call-start = ((), (), s32[]{:S(2)}) async-start(), calls=%async_computation.1 | async-start | bytes 2097152 | tf_op jit(solution)/shard_map/psum | solution.py:129
  8.8 99.0 %collective-permute-start = (bf16[2,1,8,256]{3,2,1,0:T(8,128)(2,1)S(1)}, bf16[2,1,8,256]{3,2,1,0:T(8,128)(2,1)S(1)}, u32[]{:S(2)}, u32[]{:S(2)}) collective-permute-start(bf16[2,1,8,256]{3,2,1,0:T(8,128)(2,1)S(1)} %get-tuple-element.104), channel_id=1, source_target_pairs={{0,64},{64,128},{128,192},{192,256},{256,320},{320,384},{384,448},... | collective-permute-start | bytes 24584 | tf_op jit(solution)/shard_map/ppermute | solution.py:24
  12.9 94.9 %collective-permute-start.1 = (bf16[2,1,8,256]{3,2,1,0:T(8,128)(2,1)S(1)}, bf16[2,1,8,256]{3,2,1,0:T(8,128)(2,1)S(1)}, u32[]{:S(2)}, u32[]{:S(2)}) collective-permute-start(bf16[2,1,8,256]{3,2,1,0:T(8,128)(2,1)S(1)} %get-tuple-element.105), channel_id=1, source_target_pairs={{64,0},{128,64},{192,128},{256,192},{320,256},{384,320},{448,384},... | collective-permute-start | bytes 24584 | tf_op jit(solution)/shard_map/ppermute | solution.py:25
  102.0 5.8 copy-start.9
  102.0 5.8 copy-start.10
  103.7 10.4 %copy-start.12 = (bf16[4,4,3,512]{3,1,2,0:T(4,128)(2,1)S(1)}, bf16[4,4,3,512]{3,1,2,0:T(4,128)(2,1)}, u32[]{:S(2)}) copy-start(bf16[4,4,3,512]{3,1,2,0:T(4,128)(2,1)} %param.14) | copy-start | bytes 147460
  108.6 58.9 %collective-permute-start.3 = (bf16[50,8,256]{2,1,0:T(8,128)(2,1)}, bf16[50,8,256]{2,1,0:T(8,128)(2,1)}, u32[]{:S(2)}, u32[]{:S(2)}) collective-permute-start(bf16[50,8,256]{2,1,0:T(8,128)(2,1)} %slice_bitcast_fusion.26), channel_id=1, source_target_pairs={{1,0},{2,1},{3,2},{4,3},{5,4},{6,5},{7,6},{8,7},{9,8},{10,9},{11,1... | collective-permute-start | bytes 614408 | tf_op jit(solution)/shard_map/ppermute | solution.py:25
  110.7 56.8 %collective-permute-start.2 = (bf16[50,8,256]{2,1,0:T(8,128)(2,1)}, bf16[50,8,256]{2,1,0:T(8,128)(2,1)}, u32[]{:S(2)}, u32[]{:S(2)}) collective-permute-start(bf16[50,8,256]{2,1,0:T(8,128)(2,1)} %slice_bitcast_fusion.26), channel_id=1, source_target_pairs={{0,1},{1,2},{2,3},{3,4},{4,5},{5,6},{6,7},{7,8},{8,9},{9,10},{10,1... | collective-permute-start | bytes 614408 | tf_op jit(solution)/shard_map/ppermute | solution.py:24
  167.5 3.6 copy-start.2
  167.5 3.2 copy-start.6
  169.3 1.8 copy-start.5
  171.1 2.0 copy-start.11
  174.5 466.1 %all-gather.2.cloned.1.call-start = ((), (), s32[]{:S(2)}) async-start(), calls=%async_computation | async-start | bytes 2129920 | tf_op jit(solution)/shard_map/all_gather | solution.py:137
  175.0 12.4 %copy-start.3 = (bf16[4,50,8,256]{3,2,0,1:T(8,128)(2,1)}, bf16[4,50,8,256]{3,2,0,1:T(8,128)(2,1)S(1)}, u32[]{:S(2)}) copy-start(bf16[4,50,8,256]{3,2,0,1:T(8,128)(2,1)S(1)} %fusion.13) | copy-start | bytes 2457604
  175.7 460.8 %collective-permute-start.5 = (bf16[4,50,8,256]{3,2,0,1:T(8,128)(2,1)S(1)}, bf16[4,50,8,256]{3,2,0,1:T(8,128)(2,1)}, u32[]{:S(2)}, u32[]{:S(2)}) collective-permute-start(bf16[4,50,8,256]{3,2,0,1:T(8,128)(2,1)S(1)} %fusion.13), channel_id=1, source_target_pairs={{1,0},{2,1},{3,2},{4,3},{5,4},{6,5},{7,6},{8,7},{9,8},{10,9},{11,1... | collective-permute-start | bytes 2457608 | tf_op jit(solution)/shard_map/ppermute | solution.py:25
  177.6 458.9 %collective-permute-start.4 = (bf16[4,50,8,256]{3,2,0,1:T(8,128)(2,1)S(1)}, bf16[4,50,8,256]{3,2,0,1:T(8,128)(2,1)}, u32[]{:S(2)}, u32[]{:S(2)}) collective-permute-start(bf16[4,50,8,256]{3,2,0,1:T(8,128)(2,1)S(1)} %fusion.13), channel_id=1, source_target_pairs={{0,1},{1,2},{2,3},{3,4},{4,5},{5,6},{6,7},{7,8},{8,9},{9,10},{10,1... | collective-permute-start | bytes 2457608 | tf_op jit(solution)/shard_map/ppermute | solution.py:24
  634.2 2.4 copy-start.4
  636.5 1.6 copy-start.7
  638.2 1.0 copy-start.8
  691.9 2.3 copy-start.1
Sparse Core Ops, SparseCore 0:
  174.6 459.4 all-reduce.16
Sparse Core Ops, SparseCore 1:
  178.5 130.8 all-gather.1
where the time goes:
time: 709 us; the launch traced here: 708 us
  waiting for transfers between devices  447 us (63%)
  local copies, waits for them, and re-layouts  116 us (16%)
  blocking collectives  86.1 us (12%)
  matrix products  17.9 us (3%)
  starting transfers between devices  16.7 us (2%)
  between operations  15.8 us (2%)
  other arithmetic  8.49 us (1%)
    psum x1, waiting for transfers between devices, local(): lax.psum(local_grad, ('lat', 'lon'))  447 us
    all_gather x1, blocking collectives, local(): cycle_signal = lax.all_gather(signal_slab, 'lon', axis=1, tiled=True)  86.1 us
    gather x2, local copies, waits for them, and re-layouts, polar_backward(): pole_kernel[:, :, :, (cycle_lons[None, :] - out_lons[:, None]) % lon_total]  51.2 us
    gather x2, local copies, waits for them, and re-layouts, polar_forward(): pole_kernel[:, :, :, (out_lons[:, None] - cycle_lons[None, :]) % lon_total]  50.3 us
  transfers between devices with their start and end apart: 8, of which 1 were waited for; matrix products, arithmetic and copies ran while one was open for 10% of the time, Pallas kernels for 0%

commit v1 on v0

v1 whole, which is shorter than its diff:
```python
import functools
import math

import jax
import jax.numpy as jnp
from jax import lax
from jax.experimental import pallas as pl
from jax.experimental.pallas import tpu as pltpu
from jax.sharding import PartitionSpec as P

K = 4
R = 1
H = 8
P_SIZE = 2
L = 8
SLAB = P_SIZE + R
X_HI = 2
X_LO = 2
XS = X_HI * X_LO
MESH = pl.DeviceIdType.MESH
F32 = jnp.float32
BF16 = jnp.bfloat16


def dot(a, b):
    return jnp.dot(a, b, preferred_element_type=F32)


def kernel(
    sig, cot, w_hbm, bf_hbm, bb_hbm, rev_hbm, cyc_hbm,
    conv_out, sgrad_out, wgrad_out,
    s_o, s_l, s_r, c_o, c_l, c_r, w, bf, bb, rev, cyc,
    amat, bmat, filt, grad, cot2, conv_v, sg_v,
    slab, qf, qb,
    wown, wsend, wrecv, half, xs, xr, zs, zr, za, fin, wg_v,
    load_sem, halo_ss, halo_rs, px_sem, rr_ss, rr_rs, rl_ss, rl_rs, pf_ss, pf_rs,
    core_sem, x_ss, x_rs, z_ss, z_rs, za_ss, za_rs, xa_ss, xa_rs, fc_sem, out_sem,
):
    rows, _, chans = sig.shape
    nlat, nlon = lax.axis_size("lat"), lax.axis_size("lon")
    ys, zn = nlat // X_LO, nlon // (2 * X_HI)
    lat, lon = lax.axis_index("lat"), lax.axis_index("lon")
    x_lo, y = lat // ys, lat % ys
    x_hi, z, core = lon // (2 * zn), (lon // 2) % zn, lon % 2
    x = x_hi * X_LO + x_lo
    me_q = x * ys + y
    nq = XS * ys
    blocks = rows // 8
    is_top = lat == 0
    is_polar = is_top | (lat == nlat - 1)

    def place(xx, yy, zz, cc):
        return {"lat": (xx % X_LO) * ys + yy, "lon": (xx // X_LO) * (2 * zn) + zz * 2 + cc}

    def xy_peer(o):
        xx, yy = (x + o // ys) % XS, (y + o % ys) % ys
        return xx * ys + yy, place(xx, yy, z, core)

    def z_peer(d):
        zz = (z + d) % zn
        return zz, place(x, y, zz, core)

    def beside(dlat, dlon):
        return {"lat": (lat + dlat + nlat) % nlat, "lon": (lon + dlon + nlon) % nlon}

    partner = place(x, y, z, 1 - core)

    def remote(src, dst, ss, rs, dev):
        return pltpu.make_async_remote_copy(
            src_ref=src, dst_ref=dst, send_sem=ss, recv_sem=rs, device_id=dev, device_id_type=MESH
        )

    loads = [
        pltpu.make_async_copy(a, b, load_sem.at[i])
        for i, (a, b) in enumerate((
            (bf_hbm, bf), (sig, s_o.at[pl.ds(1, rows)]), (cot, c_o.at[pl.ds(1, rows)]),
            (bb_hbm, bb), (rev_hbm, rev), (cyc_hbm, cyc), (w_hbm, w),
        ))
    ]
    for copy in loads:
        copy.start()

    barrier = pltpu.get_barrier_semaphore()

    def greet(dev):
        pl.semaphore_signal(barrier, inc=1, device_id=dev, device_id_type=MESH)

    for dlat, dlon in ((0, 1), (0, -1), (1, 1), (1, -1), (-1, 1), (-1, -1)):
        greet(beside(dlat, dlon))

    def greet_xy(o, c):
        greet(xy_peer(o)[1])
        return c

    def greet_z(d, c):
        greet(z_peer(d)[1])
        return c

    lax.fori_loop(1, nq, greet_xy, 0)
    lax.fori_loop(1, zn, greet_z, 0)
    pl.semaphore_wait(barrier, 6 + (nq - 1) + (zn - 1))

    def halo_copies(src, own, left, right, n):
        last, first = src.at[pl.ds(rows - 1, 1)], src.at[pl.ds(0, 1)]
        top, bottom = pl.ds(0, 1), pl.ds(rows + 1, 1)
        spec = (
            (src, left.at[pl.ds(1, rows)], beside(0, 1)),
            (src, right.at[pl.ds(1, rows)], beside(0, -1)),
            (last, own.at[top], beside(1, 0)),
            (last, left.at[top], beside(1, 1)),
            (last, right.at[top], beside(1, -1)),
            (first, own.at[bottom], beside(-1, 0)),
            (first, left.at[bottom], beside(-1, 1)),
            (first, right.at[bottom], beside(-1, -1)),
        )
        return [
            remote(a, b, halo_ss.at[n + i], halo_rs.at[n + i], dev)
            for i, (a, b, dev) in enumerate(spec)
        ]

    slab_at = jnp.where(is_top, 0, rows - SLAB)
    pole_at = jnp.where(is_top, 0, rows - P_SIZE)
    slab_src = (sig.at[pl.ds(slab_at, SLAB)], cot.at[pl.ds(pole_at, P_SIZE)])
    mine = (slab.at[pl.ds(0, SLAB), x_hi, z, core], slab.at[pl.ds(SLAB, P_SIZE), x_hi, z, core])
    x_other = place((x + X_LO) % XS, y, z, core)

    @pl.when(is_polar)
    def _():
        for i in range(2):
            pltpu.make_async_copy(slab_src[i], mine[i], px_sem.at[i]).start()
            remote(slab_src[i], mine[i], px_sem.at[2 + i], px_sem.at[4 + i], x_other).start()

    sig_halo = halo_copies(sig, s_o, s_l, s_r, 0)
    cot_halo = halo_copies(cot, c_o, c_l, c_r, 8)
    for copy in sig_halo + cot_halo:
        copy.start()

    def build(src, dst):
        def block(b, c):
            for k in range(K):
                tile = src[k, pl.ds(pl.multiple_of(b * 8, 8), 8), :]
                for i in range(0, 8, 2):
                    parts = [
                        pltpu.roll(
                            jnp.broadcast_to(tile[j : j + 1], (L, tile.shape[1])),
                            j * 3 * L, 1, stride=1, stride_axis=0,
                        )
                        for j in (i, i + 1)
                    ]
                    dst[b, pl.ds((k * 8 + i) * L, 2 * L), :] = jnp.concatenate(parts, 0).astype(BF16)
            return c

        lax.fori_loop(0, blocks, block, 0)

    def window(o, left, right, b):
        at = pl.ds(b * 8, 10)
        parts = [ref[at].astype(F32) for ref in (left, o, right)]
        both = jnp.concatenate(parts, 1).reshape(30 * L, chans)
        return jnp.concatenate([both, jnp.zeros((2 * L, chans), F32)], 0).astype(BF16)

    def cycle_rows(src, r):
        row = jnp.broadcast_to(src[r : r + 1, :], (L, src.shape[1]))
        return pltpu.roll(row, 0, 1, stride=1, stride_axis=0)

    loads[0].wait()
    build(bf, amat)
    loads[3].wait()
    build(bb, bmat)

    circle = nlon * L
    loads[4].wait()
    loads[5].wait()

    @pl.when(is_polar)
    def _():
        rev[...] = pltpu.roll(rev[...], lon * L, 1)
        cyc[...] = pltpu.roll(cyc[...], lon * L, 1)
        for k in range(K):
            for r in range(SLAB):
                at = (k * SLAB + r) * P_SIZE
                rows_f = [cycle_rows(rev, at + p) for p in range(P_SIZE)]
                qf[pl.ds(k * 16, 16), pl.ds(r * circle, circle)] = jnp.concatenate(rows_f, 0).astype(BF16)
        for kj in range(0, K * SLAB, 2):
            for p in range(P_SIZE):
                rows_b = [cycle_rows(cyc, (kj + t) * P_SIZE + p) for t in range(2)]
                qb[pl.ds(kj * L, 16), pl.ds(p * circle, circle)] = jnp.concatenate(rows_b, 0).astype(BF16)

    hops = zn // 2

    def block_at(b):
        return slab.at[:, :, b, core]

    def ring_right(t):
        blk = block_at((z - t + zn) % zn)
        return remote(blk, blk, rr_ss.at[t], rr_rs.at[t], z_peer(1)[1])

    def ring_left(t):
        blk = block_at((z + t) % zn)
        return remote(blk, blk, rl_ss.at[t], rl_rs.at[t], z_peer(zn - 1)[1])

    def pass_on(b, n):
        blk = block_at(b)
        return remote(blk, blk, pf_ss.at[n], pf_rs.at[n], partner)

    @pl.when(is_polar)
    def _():
        for i in range(2):
            pltpu.make_async_copy(slab_src[i], mine[i], px_sem.at[i]).wait()
        for i in range(2):
            remote(slab_src[i], mine[i], px_sem.at[2 + i], px_sem.at[4 + i], x_other).wait()

        def step(t, c):
            ring_right(t).start()

            @pl.when(t < hops - 1)
            def _():
                ring_left(t).start()

            pass_on((z - t + zn) % zn, t).start()

            @pl.when((t > 0) & (t < hops))
            def _():
                pass_on((z + t) % zn, hops + t).start()

            ring_right(t).wait_recv()

            @pl.when(t < hops - 1)
            def _():
                ring_left(t).wait_recv()

            return c

        lax.fori_loop(0, hops, step, 0)
        pass_on((z - hops + zn) % zn, hops).start()

    loads[1].wait()
    for copy in sig_halo:
        copy.wait_recv()

    def forward(b, c):
        part = dot(amat[b], window(s_o, s_l, s_r, b)).astype(BF16)
        for k in range(K):
            filt[k, pl.ds(b * 64, 64), :] = part[k * 64 : (k + 1) * 64]
        return c

    lax.fori_loop(0, blocks, forward, 0)
    loads[2].wait()

    def fold(b, c):
        cot2[pl.ds(b * 64, 64), :] = (
            c_o[pl.ds(1 + b * 8, 8)].astype(F32).reshape(64, chans).astype(BF16)
        )
        return c

    lax.fori_loop(0, blocks, fold, 0)

    def circle_of(r):
        return slab[r].astype(F32).reshape(circle, chans).astype(BF16)

    @pl.when(is_polar)
    def _():
        def step(t, c):
            pass_on((z - t + zn) % zn, t).wait()
            return c

        lax.fori_loop(0, zn, step, 0)

        def sent(t, c):
            ring_right(t).wait_send()

            @pl.when(t < hops - 1)
            def _():
                ring_left(t).wait_send()

            return c

        lax.fori_loop(0, hops, sent, 0)
        part = sum(dot(qf[:, r * circle : (r + 1) * circle], circle_of(r)) for r in range(SLAB))
        at = pl.multiple_of(jnp.where(is_top, 0, (rows - P_SIZE) * L), 16)
        for k in range(K):
            filt[k, pl.ds(at, 16), :] = part[k * 16 : (k + 1) * 16].astype(BF16)

    def weight_part(k):
        return lax.dot_general(
            filt[k], cot2[...], (((0,), (0,)), ((), ())), preferred_element_type=F32
        )

    per_core = K // 2
    for i in range(per_core):
        wsend[pl.ds(i * chans, chans), :] = weight_part((1 - core) * per_core + i).astype(BF16)
    to_core = remote(wsend, wrecv, core_sem.at[0], core_sem.at[1], partner)
    to_core.start()
    for i in range(per_core):
        wown[pl.ds(i * chans, chans), :] = weight_part(core * per_core + i)

    piece = per_core * chans // nq
    to_core.wait_recv()
    summed = wown[...] + wrecv[...].astype(F32)
    half[...] = summed.reshape(nq, piece, chans)
    xs[...] = summed.astype(BF16).reshape(nq, piece, chans)

    def xy_copy(o):
        q, dev = xy_peer(o)
        return remote(xs.at[q], xr.at[o], x_ss.at[o], x_rs.at[o], dev)

    def loop(lo, hi, f):
        def body(i, c):
            f(i)
            return c

        lax.fori_loop(lo, hi, body, 0)

    loop(1, nq, lambda o: xy_copy(o).start())

    loads[6].wait()
    chunk = 8

    def mix_out(b):
        at = pl.ds(b * chunk * L, chunk * L)
        acc = sum(dot(filt[k, at, :], w[k]) for k in range(K))
        conv_v[pl.ds(b * chunk, chunk)] = acc.reshape(chunk, L, chans).astype(BF16)

    loop(0, rows // chunk, mix_out)
    conv_copy = pltpu.make_async_copy(conv_v, conv_out, out_sem.at[0])
    conv_copy.start()

    loop(1, nq, lambda o: xy_copy(o).wait_recv())
    total = half[me_q]
    for o in range(1, nq):
        total = total + xr[o].astype(F32)
    owners = zn // 2
    tiles = piece * chans // (owners * 8 * 128)
    for t in range(owners * tiles):
        r, h = t // (chans // 128), t % (chans // 128)
        zs[t // tiles, t % tiles] = total[r * 8 : (r + 1) * 8, h * 128 : (h + 1) * 128]

    def z_copy(d):
        zz, dev = z_peer(d)
        return remote(zs.at[zz % owners], zr.at[d], z_ss.at[d], z_rs.at[d], dev)

    loop(1, zn, lambda d: z_copy(d).start())

    for copy in cot_halo:
        copy.wait_recv()

    def backward(b):
        part = dot(bmat[b], window(c_o, c_l, c_r, b))
        for k in range(K):
            grad[k, pl.ds(b * 64, 64), :] = part[k * 64 : (k + 1) * 64]

    loop(0, blocks, backward)

    loop(1, zn, lambda d: z_copy(d).wait_recv())
    zr[0] = zs[z % owners]
    acc = zr[0] + zr[owners]
    for d in range(1, owners):
        acc = acc + (zr[d] + zr[d + owners])
    za[z % owners] = acc * F32(1.0 / math.sqrt(rows * nlat * L * nlon))

    def za_copy(i):
        d = i + 1 + jnp.where(i >= owners // 2, zn - owners, 0)
        dst = za.at[z % owners]
        return remote(dst, dst, za_ss.at[i], za_rs.at[i], z_peer(d)[1])

    loop(0, owners - 1, lambda i: za_copy(i).start())

    @pl.when(is_polar)
    def _():
        extra = sum(
            dot(qb[:, p * circle : (p + 1) * circle], circle_of(SLAB + p)) for p in range(P_SIZE)
        )
        at = pl.multiple_of(jnp.where(is_top, 0, (rows - SLAB) * L), 8)
        for k in range(K):
            grad[k, pl.ds(at, SLAB * L), :] += extra[k * SLAB * L : (k + 1) * SLAB * L]

    loop(0, owners - 1, lambda i: za_copy(i).wait_recv())
    lanes = chans // 128
    lines = []
    for r in range(piece // 8):
        line = [
            za[(r * lanes + h) // tiles, (r * lanes + h) % tiles] for h in range(lanes)
        ]
        lines.append(jnp.concatenate(line, 1))
    fin[core, me_q] = jnp.concatenate(lines, 0).astype(BF16)

    def xa_copy(o):
        dst = fin.at[core, me_q]
        return remote(dst, dst, xa_ss.at[o], xa_rs.at[o], xy_peer(o)[1])

    loop(1, nq, lambda o: xa_copy(o).start())

    def mix_back(b):
        at = pl.ds(b * chunk * L, chunk * L)
        acc = sum(
            lax.dot_general(
                grad[k, at, :].astype(BF16), w[k], (((1,), (1,)), ((), ())),
                preferred_element_type=F32,
            )
            for k in range(K)
        )
        sg_v[pl.ds(b * chunk, chunk)] = acc.reshape(chunk, L, chans).astype(BF16)

    loop(0, rows // chunk, mix_back)
    sg_copy = pltpu.make_async_copy(sg_v, sgrad_out, out_sem.at[1])
    sg_copy.start()

    loop(1, nq, lambda o: xa_copy(o).wait_recv())
    swap = remote(fin.at[core], fin.at[core], fc_sem.at[0], fc_sem.at[1], partner)
    swap.start()
    half_rows = per_core * chans

    def expand(c):
        wg_v[pl.ds(pl.multiple_of(c * half_rows, 8), half_rows), :] = (
            fin[c].reshape(half_rows, chans).astype(F32)
        )

    expand(core)
    swap.wait()
    expand(1 - core)
    wg_copy = pltpu.make_async_copy(wg_v, wgrad_out, out_sem.at[2])
    wg_copy.start()

    for copy in sig_halo + cot_halo:
        copy.wait_send()
    to_core.wait_send()
    loop(1, nq, lambda o: xy_copy(o).wait_send())
    loop(1, zn, lambda d: z_copy(d).wait_send())
    loop(0, owners - 1, lambda i: za_copy(i).wait_send())
    loop(1, nq, lambda o: xa_copy(o).wait_send())
    conv_copy.wait()
    sg_copy.wait()
    wg_copy.wait()


def prepare(band_kernel, cycle_kernel, support_width, rows):
    lat, nlat = lax.axis_index("lat"), lax.axis_size("lat")
    total = rows * nlat
    first = lat * rows
    kernel_rows = lax.dynamic_slice_in_dim(
        jnp.pad(band_kernel, ((0, 0), (R, R), (0, 0), (0, 0))), first, rows + 2 * R, 1
    ).astype(F32)
    width = lax.dynamic_slice_in_dim(jnp.pad(support_width, (R, R)), first, rows + 2 * R, 0)
    ids = first - R + jnp.arange(rows + 2 * R, dtype=jnp.int32)
    offsets = jnp.abs(jnp.arange(2 * H + 1, dtype=jnp.int32) - H)
    allowed = (offsets[None, :] <= width[:, None]) & ((ids >= P_SIZE) & (ids < total - P_SIZE))[:, None]
    coeffs = jnp.where(allowed[None, :, None, :], kernel_rows, 0.0)
    grown = jnp.pad(coeffs, ((0, 0), (0, 0), (0, 0), (0, 3 * L - 2 * H - 1)))
    flipped = jnp.pad(coeffs[..., ::-1], ((0, 0), (0, 0), (0, 0), (0, 3 * L - 2 * H - 1)))
    lanes = ((0, 0), (0, 0), (0, 256 - 9 * L))
    forward = jnp.pad(flipped[:, R : R + rows].reshape(K, rows, 9 * L), lanes)
    backward = jnp.concatenate(
        [grown[:, 2 - r : 2 - r + rows, r] for r in (2, 1, 0)], -1
    )
    backward = jnp.pad(backward, lanes)
    is_top = lat == 0
    pole = lax.dynamic_slice_in_dim(cycle_kernel, jnp.where(is_top, 0, P_SIZE), P_SIZE, 1).astype(F32)
    padded = jnp.pad(pole, ((0, 0), (0, 0), (2, 2), (0, 0)))
    start = jnp.where(is_top, 3, 2)
    cyc = jnp.stack(
        [lax.dynamic_slice_in_dim(padded[:, p], start - p, SLAB, 1) for p in range(P_SIZE)], 2
    )
    cyc = cyc.reshape(K * SLAB * P_SIZE, -1)
    rev = jnp.roll(cyc[:, ::-1], 1, axis=1)
    return forward, backward, rev, cyc


def local(signal, cotangent, weights, band_kernel, cycle_kernel, support_width):
    rows, _, chans = signal.shape
    nlat, nlon = lax.axis_size("lat"), lax.axis_size("lon")
    ys, zn = nlat // X_LO, nlon // (2 * X_HI)
    nq, owners = XS * ys, zn // 2
    circle = nlon * L
    blocks, cells = rows // 8, rows * L
    piece = K * chans // (2 * nq)
    tiles = piece * chans // (owners * 8 * 128)
    forward, backward, rev, cyc = prepare(band_kernel, cycle_kernel, support_width, rows)
    dma = pltpu.SemaphoreType.DMA
    ext = (rows + 2, L, chans)
    half_rows = K * chans // 2
    scratch = (
        [pltpu.VMEM(ext, BF16)] * 6
        + [pltpu.VMEM(weights.shape, BF16), pltpu.VMEM(forward.shape, F32)]
        + [pltpu.VMEM(backward.shape, F32), pltpu.VMEM(rev.shape, F32), pltpu.VMEM(cyc.shape, F32)]
        + [pltpu.VMEM((blocks, K * 64, 256), BF16)] * 2
        + [pltpu.VMEM((K, cells, chans), BF16), pltpu.VMEM((K, cells, chans), F32)]
        + [pltpu.VMEM((cells, chans), BF16)]
        + [pltpu.VMEM((rows, L, chans), BF16)] * 2
        + [pltpu.VMEM((SLAB + P_SIZE, X_HI, zn, 2, L, chans), BF16)]
        + [pltpu.VMEM((K * P_SIZE * L, SLAB * circle), BF16)]
        + [pltpu.VMEM((K * SLAB * L, P_SIZE * circle), BF16)]
        + [pltpu.VMEM((half_rows, chans), F32)]
        + [pltpu.VMEM((half_rows, chans), BF16)] * 2
        + [pltpu.VMEM((nq, piece, chans), F32)]
        + [pltpu.VMEM((nq, piece, chans), BF16)] * 2
        + [pltpu.VMEM((owners, tiles, 8, 128), F32), pltpu.VMEM((zn, tiles, 8, 128), F32)]
        + [pltpu.VMEM((owners, tiles, 8, 128), F32)]
        + [pltpu.VMEM((2, nq, piece, chans), BF16), pltpu.VMEM((K * chans, chans), F32)]
        + [dma((n,)) for n in (
            7, 16, 16, 6, owners, owners, owners, owners, zn, zn,
            2, nq, nq, zn, zn, owners, owners, nq, nq, 2, 3,
        )]
    )
    field = jax.ShapeDtypeStruct(signal.shape, BF16)
    conv, sgrad, wgrad = pl.pallas_call(
        kernel,
        out_shape=(field, field, jax.ShapeDtypeStruct((K * chans, chans), F32)),
        in_specs=[pl.BlockSpec(memory_space=pl.ANY)] * 7,
        out_specs=[pl.BlockSpec(memory_space=pl.ANY)] * 3,
        scratch_shapes=scratch,
        compiler_params=pltpu.CompilerParams(
            collective_id=0, has_side_effects=True, vmem_limit_bytes=48 * 2**20
        ),
        cost_estimate=pl.CostEstimate(flops=10**9, bytes_accessed=4 * 10**6, transcendentals=0),
    )(signal, cotangent, weights, forward, backward, rev, cyc)
    return conv, sgrad, wgrad.reshape(K, chans, chans)


def solution(mesh):
    placed = (P("lat", "lon", None), P("lat", "lon", None), P(), P(), P(), P())
    return jax.shard_map(
        local,
        mesh=mesh,
        in_specs=placed,
        out_specs=(P("lat", "lon", None), P("lat", "lon", None), P()),
        check_vma=False,
    )
```

time: 709 us -> 92.5 us (0.13)
  waiting for transfers between devices: 447 us -> 0 us
  local copies, waits for them, and re-layouts: 116 us -> 5.55 us
  blocking collectives: 86.1 us -> 0 us
  Pallas kernels: 0 us -> 85.5 us
  matrix products: 17.9 us -> 0 us
  starting transfers between devices: 16.7 us -> 0 us
  between operations: 15.8 us -> 0.84 us
  other arithmetic: 8.49 us -> 0.47 us
    psum x1 -> x0, waiting for transfers between devices: 447 us -> none  [local(): lax.psum(local_grad, ('lat', 'lon'))]
    gather x4 -> x0, local copies, waits for them, and re-layouts: 101 us -> none  [the longest x2 51.2 us: polar_backward(): pole_kernel[:, :, :, (cycle_lons[None, :] - out_lons[:, None]) % lon_total]]
    all_gather x1 -> x0, blocking collectives: 86.1 us -> none  [local(): cycle_signal = lax.all_gather(signal_slab, 'lon', axis=1, tiled=True)]
    pallas_call x0 -> x1, Pallas kernels: none -> 85.5 us  [local(): pl.pallas_call(kernel, out_shape=(field, field, jax.ShapeDtypeStruct((K *...]
    dot_general x17 -> x0, matrix products: 17.9 us -> none  [the longest x3 4.68 us: local(): jnp.einsum('kjam,kjmc->jac', backward_mats[:, start:start + lat_count, la...]
    ppermute x6 -> x0, starting transfers between devices: 16.6 us -> none  [the longest x3 11.3 us: with_halo(): before = lax.ppermute(last, axis, up)]
    squeeze x9 -> x1, local copies, waits for them, and re-layouts: 8.88 us -> 0.03 us  [prepare(): grown[:, 2 - r:2 - r + rows, r]]
  transfers between devices with their start and end apart: 8 -> 0, of which waited for: 1 -> 0; matrix products, arithmetic and copies ran while one was open for 10% -> 0% of each run, Pallas kernels for 0% -> 0%
where the time goes in v1:
time: 92.5 us; the launch traced here: 92.3 us
  Pallas kernels  85.5 us (92%)
  local copies, waits for them, and re-layouts  5.55 us (6%)
    pallas_call x1, Pallas kernels, local(): pl.pallas_call(kernel, out_shape=(field, field, jax.ShapeDtypeStruct((K *...  85.5 us
    unnamed x16, local copies, waits for them, and re-layouts  4.05 us

profile of v1, /device:TPU:1, one launch (start us, length us, event | category | flops | bytes accessed | tf_op | source)
XLA Modules:
  0.0 92.3 jit_solution(4550399658043580966)
XLA Ops:
  0.6 0.0 copy-start
  0.6 0.0 copy-start.4
  0.7 0.8 pad_dynamic-slice_fusion.1
  1.5 0.1 compare_and_fusion
  1.6 0.0 copy-done
  1.7 0.1 fusion.3
  1.9 0.1 slice.42
  2.0 0.3 reverse.2
  2.3 0.1 slice.53
  2.4 0.1 pad_maximum_fusion.1.rev_hbm
  2.5 0.0 copy-done.4
  2.5 0.6 copy.10
  3.1 0.1 convert_select_fusion
  3.2 0.1 rev.4
  3.4 0.0 copy-start.1
  3.4 0.0 copy-start.2
  3.4 0.0 copy-start.3
  3.5 0.1 copy.11
  3.6 0.1 copy.12
  3.7 0.1 select_maximum_fusion.bb_hbm
  3.8 0.6 copy-done.1
  4.4 0.0 copy-done.2
  4.5 0.1 copy-done.3
  4.5 85.5 %shard_map.85 = (bf16[48,8,256]{2,1,0:T(8,128)(2,1)S(1)}, bf16[48,8,256]{2,1,0:T(8,128)(2,1)S(1)}, f32[1024,256]{1,0:T(8,128)S(1)}) custom-call(bf16[48,8,256]{2,1,0:T(8,128)(2,1)S(1)} %copy-done.2, bf16[48,8,256]{2,1,0:T(8,128)(2,1)S(1)} %copy-done.3, bf16[4,256,256]{2,1,0:T(8,128)(2,1)S(1)} %copy-done.1, f32[4,48,256]{2,1,0:T(8,128)S(1)} %pad.32.bf_hbm, ...), custom_call_target="tpu_custom_call" | custom-call | flops 1000000000 | bytes 4000000 | tf_op jit(solution)/shard_map/pallas_call | solution.py:504
  90.0 0.7 copy.16
  90.7 0.7 copy.17
  91.4 1.0 %copy.18 = f32[4,256,256]{2,1,0:T(8,128)} copy(f32[4,256,256]{2,1,0:T(8,128)S(1)} %bitcast.13) | data formatting | bytes 2097152
  (11 shorter events, 0.3 us)
Async XLA Ops:
  0.6 1.0 %copy-start = (bf16[4,4,3,512]{3,1,2,0:T(4,128)(2,1)S(1)}, bf16[4,4,3,512]{3,1,2,0:T(4,128)(2,1)}, u32[]{:S(2)}) copy-start(bf16[4,4,3,512]{3,1,2,0:T(4,128)(2,1)} %param.10) | copy-start | bytes 147460
  0.6 1.8 %copy-start.4 = (bf16[4,384,3,17]{1,0,3,2:T(4,128)(2,1)S(1)}, bf16[4,384,3,17]{1,0,3,2:T(4,128)(2,1)}, u32[]{:S(2)}) copy-start(bf16[4,384,3,17]{1,0,3,2:T(4,128)(2,1)} %param.9) | copy-start | bytes 470020
  3.4 1.0 %copy-start.1 = (bf16[4,256,256]{2,1,0:T(8,128)(2,1)S(1)}, bf16[4,256,256]{2,1,0:T(8,128)(2,1)}, u32[]{:S(2)}) copy-start(bf16[4,256,256]{2,1,0:T(8,128)(2,1)} %w_hbm.1) | copy-start | bytes 1572868
  3.4 1.1 %copy-start.2 = (bf16[48,8,256]{2,1,0:T(8,128)(2,1)S(1)}, bf16[48,8,256]{2,1,0:T(8,128)(2,1)}, u32[]{:S(2)}) copy-start(bf16[48,8,256]{2,1,0:T(8,128)(2,1)} %sig.1) | copy-start | bytes 589828
  3.4 1.1 %copy-start.3 = (bf16[48,8,256]{2,1,0:T(8,128)(2,1)S(1)}, bf16[48,8,256]{2,1,0:T(8,128)(2,1)}, u32[]{:S(2)}) copy-start(bf16[48,8,256]{2,1,0:T(8,128)(2,1)} %cot.1) | copy-start | bytes 589828

commit v2 on v0

v2 whole, which is shorter than its diff:
```python
import functools
import math

import jax
import jax.numpy as jnp
from jax import lax
from jax.experimental import pallas as pl
from jax.experimental.pallas import tpu as pltpu
from jax.sharding import PartitionSpec as P

K = 4
R = 1
H = 8
P_SIZE = 2
L = 8
SLAB = P_SIZE + R
X_HI = 2
X_LO = 2
XS = X_HI * X_LO
MESH = pl.DeviceIdType.MESH
F32 = jnp.float32
BF16 = jnp.bfloat16


def dot(a, b):
    return jnp.dot(a, b, preferred_element_type=F32)


def kernel(
    sig, cot, w_hbm, band_hbm, cycle_hbm, width_hbm,
    conv_out, sgrad_out, wgrad_out,
    s_o, s_l, s_r, c_o, c_l, c_r, w, band, circ, width,
    bf, bb, cyc, rev, amat, bmat, filt, grad, cot2, conv_v, sg_v,
    slab, qf, qb, gp,
    wall, wsend, wrecv, half, xs, xr, zs, zr, za, fin,
    load_sem, halo_ss, halo_rs, own_sem, pc_ss, pc_rs, px_ss, px_rs, pk_ss, pk_rs,
    ps_ss, ps_rs, pb_sem,
    core_sem, x_ss, x_rs, z_ss, z_rs, za_ss, za_rs, xa_ss, xa_rs, fc_sem, out_sem,
):
    rows, _, chans = sig.shape
    nlat, nlon = lax.axis_size("lat"), lax.axis_size("lon")
    ys, zn = nlat // X_LO, nlon // (2 * X_HI)
    lat, lon = lax.axis_index("lat"), lax.axis_index("lon")
    x_lo, y = lat // ys, lat % ys
    x_hi, z, core = lon // (2 * zn), (lon // 2) % zn, lon % 2
    x = x_hi * X_LO + x_lo
    me_q = x * ys + y
    nq = XS * ys
    blocks = rows // 8
    circle = nlon * L
    first_row, total_rows = lat * rows, rows * nlat
    is_top = lat == 0
    is_polar = is_top | (lat == nlat - 1)

    def place(xx, yy, zz, cc):
        return {"lat": (xx % X_LO) * ys + yy, "lon": (xx // X_LO) * (2 * zn) + zz * 2 + cc}

    def reach(o):
        dx, dy = o // ys, o % ys
        return min(dx, XS - dx) + min(dy, ys - dy)

    xy_order = sorted(range(1, nq), key=lambda o: -reach(o))

    def z_offset(i):
        return zn // 2 + (1 - 2 * (i % 2)) * ((i + 1) // 2)

    def xy_peer(o):
        xx, yy = (x + o // ys) % XS, (y + o % ys) % ys
        return xx * ys + yy, place(xx, yy, z, core)

    def z_peer(d):
        zz = (z + d) % zn
        return zz, place(x, y, zz, core)

    def beside(dlat, dlon):
        return {"lat": (lat + dlat + nlat) % nlat, "lon": (lon + dlon + nlon) % nlon}

    partner = place(x, y, z, 1 - core)
    x_other = place((x + X_LO) % XS, y, z, core)

    def remote(src, dst, ss, rs, dev):
        return pltpu.make_async_remote_copy(
            src_ref=src, dst_ref=dst, send_sem=ss, recv_sem=rs, device_id=dev, device_id_type=MESH
        )

    def loop(lo, hi, f):
        def body(i, c):
            f(i)
            return c

        lax.fori_loop(lo, hi, body, 0)

    barrier = pltpu.get_barrier_semaphore()

    def greet(dev):
        pl.semaphore_signal(barrier, inc=1, device_id=dev, device_id_type=MESH)

    loop(0, zn - 1, lambda i: greet(z_peer(z_offset(i))[1]))
    for o in xy_order:
        greet(xy_peer(o)[1])
    for dlat, dlon in ((1, 1), (1, -1), (-1, 1), (-1, -1), (0, 1), (0, -1)):
        greet(beside(dlat, dlon))

    def band_rows(start, n):
        return band_hbm.at[:, :, pl.ds(pl.multiple_of((start + total_rows) % total_rows, 16), n)]

    loads = [
        pltpu.make_async_copy(a, b, load_sem.at[i])
        for i, (a, b) in enumerate((
            (band_rows(first_row - 16, 16), band.at[:, :, pl.ds(0, 16)]),
            (band_rows(first_row, rows), band.at[:, :, pl.ds(16, rows)]),
            (band_rows(first_row + rows, 16), band.at[:, :, pl.ds(rows + 16, 16)]),
            (width_hbm, width),
            (cycle_hbm, circ),
            (sig, s_o.at[pl.ds(1, rows)]),
            (cot, c_o.at[pl.ds(1, rows)]),
            (w_hbm, w),
        ))
    ]
    for copy in loads:
        copy.start()
    pl.semaphore_wait(barrier, 6 + (nq - 1) + (zn - 1))

    slab_at = jnp.where(is_top, 0, rows - SLAB)
    pole_at = jnp.where(is_top, 0, rows - P_SIZE)
    sig_slab = sig.at[pl.ds(slab_at, SLAB)]
    cot_slab = cot.at[pl.ds(pole_at, P_SIZE)]
    sig_rows, cot_rows = pl.ds(0, SLAB), pl.ds(SLAB, P_SIZE)

    def cot_block(zz):
        return slab.at[cot_rows, x_hi, zz, core]

    def sig_block(zz):
        return slab.at[sig_rows, x_hi, zz, core]

    def cot_z(d):
        return remote(cot_slab, cot_block(z), pc_ss.at[d], pc_rs.at[d], z_peer(d)[1])

    def sig_z(d):
        return remote(sig_slab, sig_block(z), ps_ss.at[d], ps_rs.at[d], z_peer(d)[1])

    def cot_x(d):
        blk = cot_block((z - d + zn) % zn)
        return remote(blk, blk, px_ss.at[d], px_rs.at[d], x_other)

    def cot_core(i):
        part = slab.at[cot_rows, jnp.where(i == 0, x_hi, 1 - x_hi), :, core]
        return remote(part, part, pk_ss.at[i], pk_rs.at[i], partner)

    def sig_x():
        part = slab.at[sig_rows, x_hi, :, core]
        return remote(part, part, pb_sem.at[0], pb_sem.at[1], x_other)

    def sig_core():
        part = slab.at[sig_rows, :, :, core]
        return remote(part, part, pb_sem.at[2], pb_sem.at[3], partner)

    own_slab = [
        pltpu.make_async_copy(cot_slab, cot_block(z), own_sem.at[0]),
        pltpu.make_async_copy(sig_slab, sig_block(z), own_sem.at[1]),
    ]

    @pl.when(is_polar)
    def _():
        own_slab[0].start()
        own_slab[1].start()
        loop(0, zn - 1, lambda i: cot_z(z_offset(i)).start())

    def halo_copies(src, own, left, right, n):
        last, first = src.at[pl.ds(rows - 1, 1)], src.at[pl.ds(0, 1)]
        top, bottom = pl.ds(0, 1), pl.ds(rows + 1, 1)
        spec = (
            (last, left.at[top], beside(1, 1)),
            (last, right.at[top], beside(1, -1)),
            (first, left.at[bottom], beside(-1, 1)),
            (first, right.at[bottom], beside(-1, -1)),
            (last, own.at[top], beside(1, 0)),
            (first, own.at[bottom], beside(-1, 0)),
            (src, left.at[pl.ds(1, rows)], beside(0, 1)),
            (src, right.at[pl.ds(1, rows)], beside(0, -1)),
        )
        return [
            remote(a, b, halo_ss.at[n + i], halo_rs.at[n + i], dev)
            for i, (a, b, dev) in enumerate(spec)
        ]

    sig_halo = halo_copies(sig, s_o, s_l, s_r, 0)
    cot_halo = halo_copies(cot, c_o, c_l, c_r, 8)
    for copy in sig_halo + cot_halo:
        copy.start()

    @pl.when(is_polar)
    def _():
        own_slab[0].wait()
        cot_x(0).start()
        loop(0, zn - 1, lambda i: sig_z(z_offset(i)).start())

    for copy in loads[:4]:
        copy.wait()
    lanes = 256
    lag = lax.broadcasted_iota(jnp.int32, (2 * H + 1, lanes), 0)
    lane = lax.broadcasted_iota(jnp.int32, (2 * H + 1, lanes), 1)
    taps = range(2 * R + 1)
    table_f = [(lane == r * 3 * L + 2 * H - lag).astype(F32).astype(BF16) for r in taps]
    table_b = [(lane == (2 * R - r) * 3 * L + lag).astype(F32).astype(BF16) for r in taps]
    for k in range(K):
        taken = [band[r, k].astype(F32) for r in taps]
        bf[k] = sum(dot(taken[r][16 : 16 + rows].astype(BF16), table_f[r]) for r in taps)
        bb[k] = sum(
            dot(taken[r][17 - r : 17 - r + rows].astype(BF16), table_b[r]) for r in taps
        )
    lane_row = lax.broadcasted_iota(jnp.int32, (1, lanes), 1)
    slot = lane_row // (3 * L)
    away = jnp.abs(lane_row - slot * (3 * L) - H)

    def width_of(i):
        row = first_row + i
        held = width[(row + total_rows) % total_rows]
        return jnp.where((row >= P_SIZE) & (row < total_rows - P_SIZE), held, -1)

    def build(src, dst, backward):
        def block(b):
            allowed = []
            for i in range(8):
                row = b * 8 + i
                if backward:
                    near = [width_of(row + s - R) for s in taps]
                    limit = jnp.where(slot == 0, near[0], jnp.where(slot == 1, near[1], near[2]))
                else:
                    limit = width_of(row)
                allowed.append(away <= limit)
            for k in range(K):
                tile = src[k, pl.ds(pl.multiple_of(b * 8, 8), 8), :]
                for i in range(0, 8, 2):
                    parts = [
                        pltpu.roll(
                            jnp.broadcast_to(jnp.where(allowed[j], tile[j : j + 1], 0.0), (L, lanes)),
                            j * 3 * L, 1, stride=1, stride_axis=0,
                        )
                        for j in (i, i + 1)
                    ]
                    dst[b, pl.ds((k * 8 + i) * L, 2 * L), :] = jnp.concatenate(parts, 0).astype(BF16)

        loop(0, blocks, block)

    def window(o, left, right, b):
        at = pl.ds(b * 8, 10)
        parts = [ref[at].astype(F32) for ref in (left, o, right)]
        both = jnp.concatenate(parts, 1).reshape(30 * L, chans)
        return jnp.concatenate([both, jnp.zeros((2 * L, chans), F32)], 0).astype(BF16)

    build(bf, amat, False)

    loads[4].wait()

    def cycle_rows(src, r):
        row = jnp.broadcast_to(src[r : r + 1, :], (L, circle))
        return pltpu.roll(row, 0, 1, stride=1, stride_axis=0)

    @pl.when(is_polar)
    def _():
        none = jnp.zeros((1, circle), F32)
        for k in range(K):
            for p in range(P_SIZE):

                def tap(r):
                    if not 0 <= r <= 2 * R:
                        return none
                    held = circ[k, r].astype(F32)
                    return jnp.where(is_top, held[p : p + 1], held[P_SIZE + p : P_SIZE + p + 1])

                for r in taps:
                    at = (k * SLAB + r) * P_SIZE + p
                    cyc[at : at + 1, :] = jnp.where(is_top, tap(r - p + R), tap(r - p))
        start = cyc[...]
        from_lag = lax.broadcasted_iota(jnp.int32, (circle, circle), 0)
        to_lag = lax.broadcasted_iota(jnp.int32, (circle, circle), 1)
        turned = ((from_lag + to_lag) % circle == 0).astype(F32).astype(BF16)
        rev[...] = pltpu.roll(dot(start.astype(BF16), turned), lon * L, 1)
        cyc[...] = pltpu.roll(start, lon * L, 1)
        for kj in range(0, K * SLAB, 2):
            for p in range(P_SIZE):
                rows_b = [cycle_rows(cyc, (kj + t) * P_SIZE + p) for t in range(2)]
                qb[pl.ds(kj * L, 16), pl.ds(p * circle, circle)] = jnp.concatenate(rows_b, 0).astype(BF16)

        def pass_on(i):
            d = z_offset(zn - 2 - i)
            cot_z(d).wait_recv()
            cot_x(d).start()

        loop(0, zn - 1, pass_on)
        cot_core(0).start()

    loads[5].wait()
    for copy in sig_halo:
        copy.wait_recv()

    def forward(b):
        part = dot(amat[b], window(s_o, s_l, s_r, b)).astype(BF16)
        for k in range(K):
            filt[k, pl.ds(b * 64, 64), :] = part[k * 64 : (k + 1) * 64]

    loop(0, blocks, forward)
    loads[6].wait()

    def fold(b):
        cot2[pl.ds(b * 64, 64), :] = (
            c_o[pl.ds(1 + b * 8, 8)].astype(F32).reshape(64, chans).astype(BF16)
        )

    loop(0, blocks, fold)

    @pl.when(is_polar)
    def _():
        loop(0, zn, lambda d: cot_x(d).wait_recv())
        cot_core(1).start()

    for k in range(K):
        wall[pl.ds(k * chans, chans), :] = lax.dot_general(
            filt[k], cot2[...], (((0,), (0,)), ((), ())), preferred_element_type=F32
        )

    def circle_of(r):
        return slab[r].astype(F32).reshape(circle, chans).astype(BF16)

    @pl.when(is_polar)
    def _():
        cot_core(0).wait_recv()
        cot_core(1).wait_recv()
        gp[...] = sum(
            dot(qb[:, p * circle : (p + 1) * circle], circle_of(SLAB + p)) for p in range(P_SIZE)
        )
        near = s_o[pl.ds(slab_at + 1, SLAB)].astype(F32).reshape(SLAB * L, chans).astype(BF16)
        for k in range(K):
            wall[pl.ds(k * chans, chans), :] += lax.dot_general(
                near, gp[k * SLAB * L : (k + 1) * SLAB * L].astype(BF16),
                (((0,), (0,)), ((), ())), preferred_element_type=F32,
            )

    half_rows = K * chans // 2
    wsend[...] = wall[pl.ds(pl.multiple_of((1 - core) * half_rows, 8), half_rows), :].astype(BF16)
    to_core = remote(wsend, wrecv, core_sem.at[0], core_sem.at[1], partner)
    to_core.start()
    piece = half_rows // nq
    mine = wall[pl.ds(pl.multiple_of(core * half_rows, 8), half_rows), :]
    to_core.wait_recv()
    summed = mine + wrecv[...].astype(F32)
    half[...] = summed.reshape(nq, piece, chans)
    xs[...] = summed.astype(BF16).reshape(nq, piece, chans)

    def xy_copy(o):
        q, dev = xy_peer(o)
        return remote(xs.at[q], xr.at[o], x_ss.at[o], x_rs.at[o], dev)

    for o in xy_order:
        xy_copy(o).start()

    loads[7].wait()
    chunk = 8

    def mix_out(b):
        at = pl.ds(b * chunk * L, chunk * L)
        acc = sum(dot(filt[k, at, :], w[k]) for k in range(K))
        conv_v[pl.ds(b * chunk, chunk)] = acc.reshape(chunk, L, chans).astype(BF16)

    loop(0, rows // chunk, mix_out)
    build(bb, bmat, True)

    loop(1, nq, lambda o: xy_copy(o).wait_recv())
    total = half[me_q]
    for o in range(1, nq):
        total = total + xr[o].astype(F32)

    for p in range(4):
        zs[p] = total[
            (p // 2) * (piece // 2) : (p // 2 + 1) * (piece // 2), (p % 2) * 128 : (p % 2 + 1) * 128
        ].astype(BF16)

    def z_copy(d):
        zz, dev = z_peer(d)
        return remote(zs.at[zz % 4], zr.at[z], z_ss.at[d], z_rs.at[d], dev)

    loop(0, zn - 1, lambda i: z_copy(z_offset(i)).start())
    zr[z] = zs[z % 4]

    @pl.when(is_polar)
    def _():
        own_slab[1].wait()
        loop(0, zn - 1, lambda i: sig_z(z_offset(i)).wait_recv())
        sig_x().start()

    for copy in cot_halo:
        copy.wait_recv()

    def backward(b):
        part = dot(bmat[b], window(c_o, c_l, c_r, b))
        for k in range(K):
            grad[k, pl.ds(b * 64, 64), :] = part[k * 64 : (k + 1) * 64]

    loop(0, blocks, backward)

    @pl.when(is_polar)
    def _():
        at = pl.multiple_of(slab_at * L, 8)
        for k in range(K):
            grad[k, pl.ds(at, SLAB * L), :] += gp[k * SLAB * L : (k + 1) * SLAB * L]

    def mix_back(b):
        at = pl.ds(b * chunk * L, chunk * L)
        acc = sum(
            lax.dot_general(
                grad[k, at, :].astype(BF16), w[k], (((1,), (1,)), ((), ())),
                preferred_element_type=F32,
            )
            for k in range(K)
        )
        sg_v[pl.ds(b * chunk, chunk)] = acc.reshape(chunk, L, chans).astype(BF16)

    loop(0, rows // chunk, mix_back)
    sg_copy = pltpu.make_async_copy(sg_v, sgrad_out, out_sem.at[1])
    sg_copy.start()

    loop(0, zn - 1, lambda i: z_copy(z_offset(i)).wait_recv())
    acc = zr[0].astype(F32)
    for s in range(1, zn):
        acc = acc + zr[s].astype(F32)
    za[z % 4] = (acc * F32(1.0 / math.sqrt(total_rows * circle))).astype(BF16)
    hand = (2, 1, zn - 1)

    def za_copy(i):
        dst = za.at[z % 4]
        return remote(dst, dst, za_ss.at[i], za_rs.at[i], z_peer(hand[i])[1])

    for i in range(3):
        za_copy(i).start()

    @pl.when(is_polar)
    def _():
        sig_x().wait_recv()
        sig_core().start()

    for i in range(3):
        za_copy(i).wait_recv()
    lines = [jnp.concatenate([za[2 * i].astype(F32), za[2 * i + 1].astype(F32)], 1) for i in range(2)]
    fin[core, me_q] = jnp.concatenate(lines, 0).astype(BF16)

    def xa_copy(o):
        dst = fin.at[core, me_q]
        return remote(dst, dst, xa_ss.at[o], xa_rs.at[o], xy_peer(o)[1])

    for o in xy_order:
        xa_copy(o).start()

    @pl.when(is_polar)
    def _():
        for k in range(K):
            for r in taps:
                at = (k * SLAB + r) * P_SIZE
                rows_f = [cycle_rows(rev, at + p) for p in range(P_SIZE)]
                qf[pl.ds(k * 16, 16), pl.ds(r * circle, circle)] = jnp.concatenate(rows_f, 0).astype(BF16)
        sig_core().wait_recv()
        part = sum(dot(qf[:, r * circle : (r + 1) * circle], circle_of(r)) for r in range(SLAB))
        out = sum(dot(part[k * 16 : (k + 1) * 16].astype(BF16), w[k]) for k in range(K))
        conv_v[pl.ds(pole_at, P_SIZE)] = out.reshape(P_SIZE, L, chans).astype(BF16)

    conv_copy = pltpu.make_async_copy(conv_v, conv_out, out_sem.at[0])
    conv_copy.start()

    loop(1, nq, lambda o: xa_copy(o).wait_recv())
    swap = remote(fin.at[core], fin.at[core], fc_sem.at[0], fc_sem.at[1], partner)
    swap.start()
    wg_copies = [
        pltpu.make_async_copy(fin.at[c], wgrad_out.at[c], out_sem.at[2 + i])
        for i, c in enumerate((core, 1 - core))
    ]
    wg_copies[0].start()

    @pl.when(is_polar)
    def _():
        loop(1, zn, lambda d: cot_z(d).wait_send())
        loop(1, zn, lambda d: sig_z(d).wait_send())
        loop(0, zn, lambda d: cot_x(d).wait_send())
        cot_core(0).wait_send()
        cot_core(1).wait_send()
        sig_x().wait_send()
        sig_core().wait_send()

    for copy in sig_halo + cot_halo:
        copy.wait_send()
    to_core.wait_send()
    loop(1, nq, lambda o: xy_copy(o).wait_send())
    loop(1, zn, lambda d: z_copy(d).wait_send())
    for i in range(3):
        za_copy(i).wait_send()
    loop(1, nq, lambda o: xa_copy(o).wait_send())
    conv_copy.wait()
    sg_copy.wait()
    swap.wait()
    wg_copies[1].start()
    wg_copies[0].wait()
    wg_copies[1].wait()


def local(signal, cotangent, weights, band_kernel, cycle_kernel, support_width):
    rows, _, chans = signal.shape
    nlat, nlon = lax.axis_size("lat"), lax.axis_size("lon")
    ys, zn = nlat // X_LO, nlon // (2 * X_HI)
    nq = XS * ys
    circle = nlon * L
    blocks, cells = rows // 8, rows * L
    half_rows = K * chans // 2
    piece = half_rows // nq
    band = band_kernel.transpose(2, 0, 1, 3)
    cycle = cycle_kernel.transpose(0, 2, 1, 3)
    dma = pltpu.SemaphoreType.DMA
    ext = (rows + 2, L, chans)
    base = pltpu.VMEM((K, rows, 256), F32)
    turns = pltpu.VMEM((K * SLAB * P_SIZE, circle), F32)
    matrices = pltpu.VMEM((blocks, K * 64, 256), BF16)
    scratch = (
        [pltpu.VMEM(ext, BF16)] * 6
        + [pltpu.VMEM(weights.shape, BF16)]
        + [pltpu.VMEM((2 * R + 1, K, rows + 32, 2 * H + 1), BF16)]
        + [pltpu.VMEM((K, 2 * R + 1, 2 * P_SIZE, circle), BF16)]
        + [pltpu.SMEM(support_width.shape, jnp.int32)]
        + [base] * 2 + [turns] * 2 + [matrices] * 2
        + [pltpu.VMEM((K, cells, chans), BF16), pltpu.VMEM((K, cells, chans), F32)]
        + [pltpu.VMEM((cells, chans), BF16)]
        + [pltpu.VMEM((rows, L, chans), BF16)] * 2
        + [pltpu.VMEM((SLAB + P_SIZE, X_HI, zn, 2, L, chans), BF16)]
        + [pltpu.VMEM((K * P_SIZE * L, SLAB * circle), BF16)]
        + [pltpu.VMEM((K * SLAB * L, P_SIZE * circle), BF16)]
        + [pltpu.VMEM((K * SLAB * L, chans), F32)]
        + [pltpu.VMEM((2 * half_rows, chans), F32)]
        + [pltpu.VMEM((half_rows, chans), BF16)] * 2
        + [pltpu.VMEM((nq, piece, chans), F32)]
        + [pltpu.VMEM((nq, piece, chans), BF16)] * 2
        + [pltpu.VMEM((n, piece // 2, 128), BF16) for n in (4, zn, 4)]
        + [pltpu.VMEM((2, nq, piece, chans), BF16)]
        + [dma((n,)) for n in (
            8, 16, 16, 2, zn, zn, zn, zn, 2, 2,
            zn, zn, 4,
            2, nq, nq, zn, zn, 3, 3, nq, nq, 2, 4,
        )]
    )
    field = jax.ShapeDtypeStruct(signal.shape, BF16)
    conv, sgrad, wgrad = pl.pallas_call(
        kernel,
        out_shape=(field, field, jax.ShapeDtypeStruct((2, nq, piece, chans), BF16)),
        in_specs=[pl.BlockSpec(memory_space=pl.ANY)] * 6,
        out_specs=[pl.BlockSpec(memory_space=pl.ANY)] * 3,
        scratch_shapes=scratch,
        compiler_params=pltpu.CompilerParams(
            collective_id=0, has_side_effects=True, vmem_limit_bytes=40 * 2**20
        ),
        cost_estimate=pl.CostEstimate(flops=10**9, bytes_accessed=4 * 10**6, transcendentals=0),
    )(signal, cotangent, weights, band, cycle, support_width)
    return conv, sgrad, wgrad.astype(F32).reshape(K, chans, chans)


def solution(mesh):
    placed = (P("lat", "lon", None), P("lat", "lon", None), P(), P(), P(), P())
    return jax.shard_map(
        local,
        mesh=mesh,
        in_specs=placed,
        out_specs=(P("lat", "lon", None), P("lat", "lon", None), P()),
        check_vma=False,
    )
```

time: 709 us -> 65.7 us (0.09)
  waiting for transfers between devices: 447 us -> 0 us
  local copies, waits for them, and re-layouts: 116 us -> 2.98 us
  blocking collectives: 86.1 us -> 0 us
  Pallas kernels: 0 us -> 60.8 us
  matrix products: 17.9 us -> 0 us
  starting transfers between devices: 16.7 us -> 0 us
  between operations: 15.8 us -> 0.73 us
  other arithmetic: 8.49 us -> 1.06 us
    psum x1 -> x0, waiting for transfers between devices: 447 us -> none  [local(): lax.psum(local_grad, ('lat', 'lon'))]
    gather x4 -> x0, local copies, waits for them, and re-layouts: 101 us -> none  [the longest x2 51.2 us: polar_backward(): pole_kernel[:, :, :, (cycle_lons[None, :] - out_lons[:, None]) % lon_total]]
    all_gather x1 -> x0, blocking collectives: 86.1 us -> none  [local(): cycle_signal = lax.all_gather(signal_slab, 'lon', axis=1, tiled=True)]
    pallas_call x0 -> x1, Pallas kernels: none -> 60.8 us  [local(): pl.pallas_call(kernel, out_shape=(field, field, jax.ShapeDtypeStruct((2,...]
    dot_general x17 -> x0, matrix products: 17.9 us -> none  [the longest x3 4.68 us: local(): jnp.einsum('kjam,kjmc->jac', backward_mats[:, start:start + lat_count, la...]
    ppermute x6 -> x0, starting transfers between devices: 16.6 us -> none  [the longest x3 11.3 us: with_halo(): before = lax.ppermute(last, axis, up)]
    squeeze x9 -> x0, local copies, waits for them, and re-layouts: 8.88 us -> none  [the longest x4 4.16 us: local(): backward_mats[:, start:start + lat_count, lat_tap]]
  transfers between devices with their start and end apart: 8 -> 0, of which waited for: 1 -> 0; matrix products, arithmetic and copies ran while one was open for 10% -> 0% of each run, Pallas kernels for 0% -> 0%
where the time goes in v2:
time: 65.7 us; the launch traced here: 65.5 us
  Pallas kernels  60.8 us (93%)
  local copies, waits for them, and re-layouts  2.98 us (5%)
  other arithmetic  1.06 us (2%)
  between operations  0.73 us (1%)
    pallas_call x1, Pallas kernels, local(): pl.pallas_call(kernel, out_shape=(field, field, jax.ShapeDtypeStruct((2,...  60.8 us
    unnamed x13, local copies, waits for them, and re-layouts  2.98 us

profile of v2, /device:TPU:1, one launch (start us, length us, event | category | flops | bytes accessed | tf_op | source)
XLA Modules:
  0.0 65.5 jit_solution(13727023551471005744)
XLA Ops:
  0.6 0.0 copy-start.4
  0.6 0.0 copy-start.3
  0.7 0.0 copy-start
  0.7 0.0 copy-start.2
  0.7 0.0 copy-start.1
  0.7 1.6 %copy.9 = bf16[4,384,3,17]{3,1,0,2:T(8,128)(2,1)S(1)} copy(bf16[4,384,3,17]{1,0,3,2:T(4,128)(2,1)} %param.9) | data formatting | bytes 313344 | tf_op args[3]
  2.3 0.0 copy-done.4
  2.3 0.0 copy-done.3
  2.3 0.0 copy-done
  2.3 0.0 copy-done.2
  2.3 0.0 copy-done.1
  2.3 60.8 %shard_map.85 = (bf16[48,8,256]{2,1,0:T(8,128)(2,1)S(1)}, bf16[48,8,256]{2,1,0:T(8,128)(2,1)S(1)}, bf16[2,16,32,256]{3,2,1,0:T(8,128)(2,1)S(1)}) custom-call(bf16[48,8,256]{2,1,0:T(8,128)(2,1)S(1)} %copy-done.1, bf16[48,8,256]{2,1,0:T(8,128)(2,1)S(1)} %copy-done.2, bf16[4,256,256]{2,1,0:T(8,128)(2,1)S(1)} %copy-done, bf16[3,4,384,17]{3,2,1,0:T(8,128)(2,1)S(1)} %bitcast.4, ...), custom_call_target="tpu_custom_call" | custom-call | flops 1000000000 | bytes 4000000 | tf_op jit(solution)/shard_map/pallas_call | solution.py:547
  63.1 1.1 %convert.1 = f32[4,256,256]{2,1,0:T(8,128)} convert(bf16[4,256,256]{2,1,0:T(8,128)(2,1)S(1)} %bitcast.5) | non-fusion elementwise | flops 262144 | bytes 1572864 | tf_op jit(solution)/shard_map/reshape | solution.py:558
  64.2 0.7 %copy.12 = bf16[48,8,256]{2,1,0:T(8,128)(2,1)} copy(bf16[48,8,256]{2,1,0:T(8,128)(2,1)S(1)} %get-tuple-element.12) | data formatting | bytes 393216
  64.9 0.7 %copy.13 = bf16[48,8,256]{2,1,0:T(8,128)(2,1)} copy(bf16[48,8,256]{2,1,0:T(8,128)(2,1)S(1)} %get-tuple-element.13) | data formatting | bytes 393216
Async XLA Ops:
  0.6 1.7 %copy-start.4 = (s32[384]{0:T(512)S(1)}, s32[384]{0:T(512)}, u32[]{:S(2)}) copy-start(s32[384]{0:T(512)} %width_hbm.1) | copy-start | bytes 4612
  0.6 1.7 %copy-start.3 = (bf16[4,4,3,512]{3,1,2,0:T(4,128)(2,1)S(1)}, bf16[4,4,3,512]{3,1,2,0:T(4,128)(2,1)}, u32[]{:S(2)}) copy-start(bf16[4,4,3,512]{3,1,2,0:T(4,128)(2,1)} %param.10) | copy-start | bytes 147460
  0.7 1.7 %copy-start = (bf16[4,256,256]{2,1,0:T(8,128)(2,1)S(1)}, bf16[4,256,256]{2,1,0:T(8,128)(2,1)}, u32[]{:S(2)}) copy-start(bf16[4,256,256]{2,1,0:T(8,128)(2,1)} %w_hbm.1) | copy-start | bytes 1572868
  0.7 1.7 %copy-start.2 = (bf16[48,8,256]{2,1,0:T(8,128)(2,1)S(1)}, bf16[48,8,256]{2,1,0:T(8,128)(2,1)}, u32[]{:S(2)}) copy-start(bf16[48,8,256]{2,1,0:T(8,128)(2,1)} %cot.1) | copy-start | bytes 589828
  0.7 1.7 %copy-start.1 = (bf16[48,8,256]{2,1,0:T(8,128)(2,1)S(1)}, bf16[48,8,256]{2,1,0:T(8,128)(2,1)}, u32[]{:S(2)}) copy-start(bf16[48,8,256]{2,1,0:T(8,128)(2,1)} %sig.1) | copy-start | bytes 589828

commit v3 on v2

--- a/solution.py
+++ b/solution.py
@@ -29,12 +29,12 @@
 def kernel(
     sig, cot, w_hbm, band_hbm, cycle_hbm, width_hbm,
     conv_out, sgrad_out, wgrad_out,
-    s_o, s_l, s_r, c_o, c_l, c_r, w, band, circ, width,
+    s_o, s_l, s_r, c_o, c_l, c_r, w, band, circ, width, taps_v, taps_t,
     bf, bb, cyc, rev, amat, bmat, filt, grad, cot2, conv_v, sg_v,
-    slab, qf, qb, gp,
+    slab, qf, qb, qt, gw, sw, part_s, part_r, own_part,
     wall, wsend, wrecv, half, xs, xr, zs, zr, za, fin,
-    load_sem, halo_ss, halo_rs, own_sem, pc_ss, pc_rs, px_ss, px_rs, pk_ss, pk_rs,
-    ps_ss, ps_rs, pb_sem,
+    far_sem, load_sem, halo_ss, halo_rs, own_sem, pc_ss, pc_rs, px_ss, px_rs, pk_sem,
+    ps_ss, ps_rs, pb_ss, pb_rs, pp_sem,
     core_sem, x_ss, x_rs, z_ss, z_rs, za_ss, za_rs, xa_ss, xa_rs, fc_sem, out_sem,
 ):
     rows, _, chans = sig.shape
@@ -61,8 +61,12 @@
 
     xy_order = sorted(range(1, nq), key=lambda o: -reach(o))
 
+    near, mid = zn // 4, zn // 2
+
     def z_offset(i):
-        return zn // 2 + (1 - 2 * (i % 2)) * ((i + 1) // 2)
+        return mid + (1 - 2 * (i % 2)) * ((i + 1) // 2)
+
+    near_order = [d for n in range(near, 0, -1) for d in (n, zn - n)]
 
     def xy_peer(o):
         xx, yy = (x + o // ys) % XS, (y + o % ys) % ys
@@ -95,21 +99,22 @@
     def greet(dev):
         pl.semaphore_signal(barrier, inc=1, device_id=dev, device_id_type=MESH)
 
-    loop(0, zn - 1, lambda i: greet(z_peer(z_offset(i))[1]))
+    for d in near_order:
+        greet(z_peer(d)[1])
+    @pl.when(is_polar)
+    def _():
+        for d in near_order:
+            greet(place((x + X_LO) % XS, y, (z + d) % zn, core))
+
     for o in xy_order:
         greet(xy_peer(o)[1])
     for dlat, dlon in ((1, 1), (1, -1), (-1, 1), (-1, -1), (0, 1), (0, -1)):
         greet(beside(dlat, dlon))
 
-    def band_rows(start, n):
-        return band_hbm.at[:, :, pl.ds(pl.multiple_of((start + total_rows) % total_rows, 16), n)]
-
     loads = [
         pltpu.make_async_copy(a, b, load_sem.at[i])
         for i, (a, b) in enumerate((
-            (band_rows(first_row - 16, 16), band.at[:, :, pl.ds(0, 16)]),
-            (band_rows(first_row, rows), band.at[:, :, pl.ds(16, rows)]),
-            (band_rows(first_row + rows, 16), band.at[:, :, pl.ds(rows + 16, 16)]),
+            (band_hbm, band),
             (width_hbm, width),
             (cycle_hbm, circ),
             (sig, s_o.at[pl.ds(1, rows)]),
@@ -119,7 +124,10 @@
     ]
     for copy in loads:
         copy.start()
-    pl.semaphore_wait(barrier, 6 + (nq - 1) + (zn - 1))
+    greeted = 6 + (nq - 1) + 2 * near
+    pl.semaphore_wait(barrier, jnp.where(is_polar, greeted + 2 * near, greeted))
+    for i, d in enumerate((near, zn - near)):
+        pl.semaphore_signal(far_sem.at[i], inc=1, device_id=z_peer(d)[1], device_id_type=MESH)
 
     slab_at = jnp.where(is_top, 0, rows - SLAB)
     pole_at = jnp.where(is_top, 0, rows - P_SIZE)
@@ -127,44 +135,63 @@
     cot_slab = cot.at[pl.ds(pole_at, P_SIZE)]
     sig_rows, cot_rows = pl.ds(0, SLAB), pl.ds(SLAB, P_SIZE)
 
-    def cot_block(zz):
-        return slab.at[cot_rows, x_hi, zz, core]
-
-    def sig_block(zz):
-        return slab.at[sig_rows, x_hi, zz, core]
+    def seen(d):
+        return mid - d if d <= mid else mid + zn - d
 
     def cot_z(d):
-        return remote(cot_slab, cot_block(z), pc_ss.at[d], pc_rs.at[d], z_peer(d)[1])
+        dst = slab.at[cot_rows, x_hi, seen(d), core]
+        return remote(cot_slab, dst, pc_ss.at[d], pc_rs.at[d], z_peer(d)[1])
 
     def sig_z(d):
-        return remote(sig_slab, sig_block(z), ps_ss.at[d], ps_rs.at[d], z_peer(d)[1])
+        dst = slab.at[sig_rows, x_hi, seen(d), core]
+        return remote(sig_slab, dst, ps_ss.at[d], ps_rs.at[d], z_peer(d)[1])
 
     def cot_x(d):
-        blk = cot_block((z - d + zn) % zn)
-        return remote(blk, blk, px_ss.at[d], px_rs.at[d], x_other)
-
-    def cot_core(i):
-        part = slab.at[cot_rows, jnp.where(i == 0, x_hi, 1 - x_hi), :, core]
-        return remote(part, part, pk_ss.at[i], pk_rs.at[i], partner)
-
-    def sig_x():
-        part = slab.at[sig_rows, x_hi, :, core]
-        return remote(part, part, pb_sem.at[0], pb_sem.at[1], x_other)
-
-    def sig_core():
-        part = slab.at[sig_rows, :, :, core]
-        return remote(part, part, pb_sem.at[2], pb_sem.at[3], partner)
+        dst = slab.at[cot_rows, x_hi, seen(d), core]
+        dev = place((x + X_LO) % XS, y, (z + d) % zn, core)
+        return remote(cot_slab, dst, px_ss.at[d], px_rs.at[d], dev)
+
+    def cot_core():
+        part = slab.at[cot_rows, :, pl.ds(mid - near, 2 * near + 1), core]
+        return remote(part, part, pk_sem.at[0], pk_sem.at[1], partner)
+
+    def far_copy(i):
+        src, dst, n, d = (
+            (mid - near, 0, near, near), (mid + 1, mid + near + 1, near - 1, zn - near)
+        )[i]
+        return remote(
+            slab.at[:, x_hi, pl.ds(src, n), core], slab.at[:, x_hi, pl.ds(dst, n), core],
+            ps_ss.at[zn + i], ps_rs.at[zn + i], z_peer(d)[1],
+        )
+
+    fars = [0, 1] if near > 1 else [0]
+    spans = [(cot_rows, 0, mid - near), (cot_rows, mid + near + 1, mid - near - 1), (sig_rows, 0, zn)]
+    spans = [span for span in spans if span[2] > 0]
+
+    def rest_core(i):
+        held, lo, n = spans[i]
+        part = slab.at[held, x_hi, pl.ds(lo, n), core]
+        return remote(part, part, pb_ss.at[i], pb_rs.at[i], partner)
+
+    def part_copy():
+        return remote(part_s, part_r, pp_sem.at[0], pp_sem.at[1], x_other)
 
     own_slab = [
-        pltpu.make_async_copy(cot_slab, cot_block(z), own_sem.at[0]),
-        pltpu.make_async_copy(sig_slab, sig_block(z), own_sem.at[1]),
+        pltpu.make_async_copy(cot_slab, slab.at[cot_rows, x_hi, mid, core], own_sem.at[0]),
+        pltpu.make_async_copy(sig_slab, slab.at[sig_rows, x_hi, mid, core], own_sem.at[1]),
     ]
 
     @pl.when(is_polar)
     def _():
         own_slab[0].start()
         own_slab[1].start()
-        loop(0, zn - 1, lambda i: cot_z(z_offset(i)).start())
+        for d in near_order:
+            cot_x(d).start()
+        for d in near_order:
+            cot_z(d).start()
+        cot_x(0).start()
+        for d in near_order:
+            sig_z(d).start()
 
     def halo_copies(src, own, left, right, n):
         last, first = src.at[pl.ds(rows - 1, 1)], src.at[pl.ds(0, 1)]
@@ -189,26 +216,34 @@
     for copy in sig_halo + cot_halo:
         copy.start()
 
-    @pl.when(is_polar)
-    def _():
-        own_slab[0].wait()
-        cot_x(0).start()
-        loop(0, zn - 1, lambda i: sig_z(z_offset(i)).start())
-
-    for copy in loads[:4]:
-        copy.wait()
+    loads[0].wait()
+    loads[1].wait()
     lanes = 256
-    lag = lax.broadcasted_iota(jnp.int32, (2 * H + 1, lanes), 0)
-    lane = lax.broadcasted_iota(jnp.int32, (2 * H + 1, lanes), 1)
     taps = range(2 * R + 1)
-    table_f = [(lane == r * 3 * L + 2 * H - lag).astype(F32).astype(BF16) for r in taps]
-    table_b = [(lane == (2 * R - r) * 3 * L + lag).astype(F32).astype(BF16) for r in taps]
+    lags = 2 * H + 1
+    used = (2 * R + 1) * lags * K
+    taps_v[...] = jnp.zeros_like(taps_v)
+    for r in taps:
+        for d in range(lags):
+            taps_v[pl.ds((r * lags + d) * K, K), :] = band[r, d].astype(F32)
+    taps_t[pl.ds(0, 16), :] = jnp.zeros((16, lanes), BF16)
+    taps_t[pl.ds(16, total_rows), :] = jnp.transpose(taps_v[...])[:total_rows].astype(BF16)
+    taps_t[pl.ds(16 + total_rows, 16), :] = jnp.zeros((16, lanes), BF16)
+    mine = taps_t[pl.ds(pl.multiple_of(first_row, 16), rows + 32), :]
+    held = lax.broadcasted_iota(jnp.int32, (lanes, 1), 0)
+    held_k, held_r, held_d = held % K, held // (K * lags), held // K % lags
+    lane = lax.broadcasted_iota(jnp.int32, (lanes, lanes), 1)
+    to_f = jnp.where(held < used, held_r * 3 * L + 2 * H - held_d, -1)
+    to_b = jnp.where(held < used, (2 * R - held_r) * 3 * L + held_d, -1)
     for k in range(K):
-        taken = [band[r, k].astype(F32) for r in taps]
-        bf[k] = sum(dot(taken[r][16 : 16 + rows].astype(BF16), table_f[r]) for r in taps)
-        bb[k] = sum(
-            dot(taken[r][17 - r : 17 - r + rows].astype(BF16), table_b[r]) for r in taps
-        )
+        placed = [
+            dot(mine, (lane == jnp.where(held_k == k, to, -1)).astype(F32).astype(BF16))
+            for to in (to_f, to_b)
+        ]
+        bf[k] = placed[0][16 : 16 + rows]
+        slots = lax.broadcasted_iota(jnp.int32, (1, lanes), 1) // (3 * L)
+        above, same, below = (placed[1][15 + s : 15 + s + rows] for s in taps)
+        bb[k] = jnp.where(slots == 0, above, jnp.where(slots == 1, same, below))
     lane_row = lax.broadcasted_iota(jnp.int32, (1, lanes), 1)
     slot = lane_row // (3 * L)
     away = jnp.abs(lane_row - slot * (3 * L) - H)
@@ -251,7 +286,7 @@
 
     build(bf, amat, False)
 
-    loads[4].wait()
+    loads[2].wait()
 
     def cycle_rows(src, r):
         row = jnp.broadcast_to(src[r : r + 1, :], (L, circle))
@@ -272,26 +307,24 @@
                 for r in taps:
                     at = (k * SLAB + r) * P_SIZE + p
                     cyc[at : at + 1, :] = jnp.where(is_top, tap(r - p + R), tap(r - p))
-        start = cyc[...]
-        from_lag = lax.broadcasted_iota(jnp.int32, (circle, circle), 0)
-        to_lag = lax.broadcasted_iota(jnp.int32, (circle, circle), 1)
-        turned = ((from_lag + to_lag) % circle == 0).astype(F32).astype(BF16)
-        rev[...] = pltpu.roll(dot(start.astype(BF16), turned), lon * L, 1)
-        cyc[...] = pltpu.roll(start, lon * L, 1)
-        for kj in range(0, K * SLAB, 2):
-            for p in range(P_SIZE):
-                rows_b = [cycle_rows(cyc, (kj + t) * P_SIZE + p) for t in range(2)]
-                qb[pl.ds(kj * L, 16), pl.ds(p * circle, circle)] = jnp.concatenate(rows_b, 0).astype(BF16)
-
-        def pass_on(i):
-            d = z_offset(zn - 2 - i)
+        col = lax.broadcasted_iota(jnp.int32, (1, circle), 1)
+        t, c = col // (8 * L) - near, col % (8 * L)
+        xh, o, cc, l = c // (4 * L), c // (2 * L) % 2, c // L % 2, c % L
+        z_cot, z_sig = (z + t + o + zn) % zn, (z - t + zn) % zn
+        lag = (xh - x_hi) * (circle // 2) + (z_cot - z_sig) * (2 * L) + (cc - core) * L + l
+        lag = (lag + 2 * circle) % circle
+        pick = (lax.broadcasted_iota(jnp.int32, (circle, circle), 0) == lag).astype(F32).astype(BF16)
+        for p in range(P_SIZE):
+            turned = [cycle_rows(cyc, n * P_SIZE + p) for n in range(K * SLAB)]
+            qt[p] = dot(jnp.concatenate(turned, 0).astype(BF16), pick).astype(BF16)
+        own_slab[0].wait()
+        for d in near_order:
             cot_z(d).wait_recv()
-            cot_x(d).start()
-
-        loop(0, zn - 1, pass_on)
-        cot_core(0).start()
-
-    loads[5].wait()
+        for d in [0] + near_order:
+            cot_x(d).wait_recv()
+        cot_core().start()
+
+    loads[3].wait()
     for copy in sig_halo:
         copy.wait_recv()
 
@@ -301,7 +334,7 @@
             filt[k, pl.ds(b * 64, 64), :] = part[k * 64 : (k + 1) * 64]
 
     loop(0, blocks, forward)
-    loads[6].wait()
+    loads[4].wait()
 
     def fold(b):
         cot2[pl.ds(b * 64, 64), :] = (
@@ -310,30 +343,36 @@
 
     loop(0, blocks, fold)
 
-    @pl.when(is_polar)
-    def _():
-        loop(0, zn, lambda d: cot_x(d).wait_recv())
-        cot_core(1).start()
-
     for k in range(K):
         wall[pl.ds(k * chans, chans), :] = lax.dot_general(
             filt[k], cot2[...], (((0,), (0,)), ((), ())), preferred_element_type=F32
         )
 
-    def circle_of(r):
-        return slab[r].astype(F32).reshape(circle, chans).astype(BF16)
-
-    @pl.when(is_polar)
-    def _():
-        cot_core(0).wait_recv()
-        cot_core(1).wait_recv()
-        gp[...] = sum(
-            dot(qb[:, p * circle : (p + 1) * circle], circle_of(SLAB + p)) for p in range(P_SIZE)
-        )
-        near = s_o[pl.ds(slab_at + 1, SLAB)].astype(F32).reshape(SLAB * L, chans).astype(BF16)
+    def cells(ref):
+        held = ref.astype(F32)
+        return held.reshape(-1, chans)
+
+    @pl.when(is_polar)
+    def _():
+        own_slab[1].wait()
+        for d in near_order:
+            sig_z(d).wait_recv()
+        cot_core().wait_recv()
+        for i in range(2 * near):
+            t = i - near
+            turned = sum(
+                dot(
+                    qt[p, :, i * 8 * L : (i + 1) * 8 * L],
+                    cells(slab[SLAB + p, :, mid + t : mid + t + 2]).astype(BF16),
+                )
+                for p in range(P_SIZE)
+            )
+            for k in range(K):
+                gw[k, pl.ds(i * SLAB * L, SLAB * L), :] = turned[k * SLAB * L : (k + 1) * SLAB * L]
+            sw[pl.ds(i * SLAB * L, SLAB * L), :] = cells(slab[0:SLAB, x_hi, mid - t, core])
         for k in range(K):
             wall[pl.ds(k * chans, chans), :] += lax.dot_general(
-                near, gp[k * SLAB * L : (k + 1) * SLAB * L].astype(BF16),
+                sw[...].astype(BF16), gw[k].astype(BF16),
                 (((0,), (0,)), ((), ())), preferred_element_type=F32,
             )
 
@@ -355,7 +394,15 @@
     for o in xy_order:
         xy_copy(o).start()
 
-    loads[7].wait()
+    @pl.when(is_polar)
+    def _():
+        for i in fars:
+            far_copy(i).start()
+
+    for i in range(2):
+        pl.semaphore_wait(far_sem.at[i], 1)
+
+    loads[5].wait()
     chunk = 8
 
     def mix_out(b):
@@ -366,6 +413,16 @@
     loop(0, rows // chunk, mix_out)
     build(bb, bmat, True)
 
+    for copy in cot_halo:
+        copy.wait_recv()
+
+    def backward(b):
+        part = dot(bmat[b], window(c_o, c_l, c_r, b))
+        for k in range(K):
+            grad[k, pl.ds(b * 64, 64), :] = part[k * 64 : (k + 1) * 64]
+
+    loop(0, blocks, backward)
+
     loop(1, nq, lambda o: xy_copy(o).wait_recv())
     total = half[me_q]
     for o in range(1, nq):
@@ -385,25 +442,10 @@
 
     @pl.when(is_polar)
     def _():
-        own_slab[1].wait()
-        loop(0, zn - 1, lambda i: sig_z(z_offset(i)).wait_recv())
-        sig_x().start()
-
-    for copy in cot_halo:
-        copy.wait_recv()
-
-    def backward(b):
-        part = dot(bmat[b], window(c_o, c_l, c_r, b))
-        for k in range(K):
-            grad[k, pl.ds(b * 64, 64), :] = part[k * 64 : (k + 1) * 64]
-
-    loop(0, blocks, backward)
-
-    @pl.when(is_polar)
-    def _():
-        at = pl.multiple_of(slab_at * L, 8)
-        for k in range(K):
-            grad[k, pl.ds(at, SLAB * L), :] += gp[k * SLAB * L : (k + 1) * SLAB * L]
+        for i in fars:
+            far_copy(i).wait_recv()
+        for i in range(len(spans)):
+            rest_core(i).start()
 
     def mix_back(b):
         at = pl.ds(b * chunk * L, chunk * L)
@@ -417,8 +459,45 @@
         sg_v[pl.ds(b * chunk, chunk)] = acc.reshape(chunk, L, chans).astype(BF16)
 
     loop(0, rows // chunk, mix_back)
-    sg_copy = pltpu.make_async_copy(sg_v, sgrad_out, out_sem.at[1])
-    sg_copy.start()
+
+    @pl.when(is_polar)
+    def _():
+        start = cyc[...]
+        from_lag = lax.broadcasted_iota(jnp.int32, (circle, circle), 0)
+        to_lag = lax.broadcasted_iota(jnp.int32, (circle, circle), 1)
+        turned = ((from_lag + to_lag) % circle == 0).astype(F32).astype(BF16)
+        rev[...] = pltpu.roll(dot(start.astype(BF16), turned), lon * L, 1)
+        cyc[...] = pltpu.roll(start, lon * L, 1)
+        side = circle // 2
+        shift = (side + (mid - z) * 2 * L) % side
+
+        def circulant(src, rows_of, dst, at):
+            full = jnp.concatenate([cycle_rows(src, n) for n in rows_of], 0)
+            for h in range(2):
+                turned_side = pltpu.roll(full[:, h * side : (h + 1) * side], shift, 1)
+                dst[h, :, pl.ds(at, side)] = turned_side.astype(BF16)
+
+        for p in range(P_SIZE):
+            circulant(cyc, [n * P_SIZE + p for n in range(K * SLAB)], qb, p * side)
+        for r in taps:
+            circulant(
+                rev, [(k * SLAB + r) * P_SIZE + p for k in range(K) for p in range(P_SIZE)], qf, r * side
+            )
+
+        for i in range(len(spans)):
+            rest_core(i).wait_recv()
+        held_rows = [cells(slab[r, x_hi]).astype(BF16) for r in range(SLAB + P_SIZE)]
+
+        def share(h):
+            front = sum(dot(qf[h, :, r * side : (r + 1) * side], held_rows[r]) for r in range(SLAB))
+            back = sum(
+                dot(qb[h, :, p * side : (p + 1) * side], held_rows[SLAB + p]) for p in range(P_SIZE)
+            )
+            return jnp.concatenate([front, back], 0)
+
+        part_s[...] = share(1 - x_hi).astype(BF16)
+        part_copy().start()
+        own_part[...] = share(x_hi)
 
     loop(0, zn - 1, lambda i: z_copy(z_offset(i)).wait_recv())
     acc = zr[0].astype(F32)
@@ -434,11 +513,6 @@
     for i in range(3):
         za_copy(i).start()
 
-    @pl.when(is_polar)
-    def _():
-        sig_x().wait_recv()
-        sig_core().start()
-
     for i in range(3):
         za_copy(i).wait_recv()
     lines = [jnp.concatenate([za[2 * i].astype(F32), za[2 * i + 1].astype(F32)], 1) for i in range(2)]
@@ -453,16 +527,23 @@
 
     @pl.when(is_polar)
     def _():
-        for k in range(K):
-            for r in taps:
-                at = (k * SLAB + r) * P_SIZE
-                rows_f = [cycle_rows(rev, at + p) for p in range(P_SIZE)]
-                qf[pl.ds(k * 16, 16), pl.ds(r * circle, circle)] = jnp.concatenate(rows_f, 0).astype(BF16)
-        sig_core().wait_recv()
-        part = sum(dot(qf[:, r * circle : (r + 1) * circle], circle_of(r)) for r in range(SLAB))
-        out = sum(dot(part[k * 16 : (k + 1) * 16].astype(BF16), w[k]) for k in range(K))
+        part_copy().wait_recv()
+        sums = own_part[...] + part_r[...].astype(F32)
+        front, extra = sums[: K * P_SIZE * L], sums[K * P_SIZE * L :]
+        out = sum(dot(front[k * 16 : (k + 1) * 16].astype(BF16), w[k]) for k in range(K))
         conv_v[pl.ds(pole_at, P_SIZE)] = out.reshape(P_SIZE, L, chans).astype(BF16)
-
+        at = pl.multiple_of(slab_at * L, 8)
+        back = sum(
+            lax.dot_general(
+                (grad[k, pl.ds(at, SLAB * L), :] + extra[k * SLAB * L : (k + 1) * SLAB * L]).astype(BF16),
+                w[k], (((1,), (1,)), ((), ())), preferred_element_type=F32,
+            )
+            for k in range(K)
+        )
+        sg_v[pl.ds(slab_at, SLAB)] = back.reshape(SLAB, L, chans).astype(BF16)
+
+    sg_copy = pltpu.make_async_copy(sg_v, sgrad_out, out_sem.at[1])
+    sg_copy.start()
     conv_copy = pltpu.make_async_copy(conv_v, conv_out, out_sem.at[0])
     conv_copy.start()
 
@@ -477,13 +558,17 @@
 
     @pl.when(is_polar)
     def _():
-        loop(1, zn, lambda d: cot_z(d).wait_send())
-        loop(1, zn, lambda d: sig_z(d).wait_send())
-        loop(0, zn, lambda d: cot_x(d).wait_send())
-        cot_core(0).wait_send()
-        cot_core(1).wait_send()
-        sig_x().wait_send()
-        sig_core().wait_send()
+        for d in near_order:
+            cot_z(d).wait_send()
+            sig_z(d).wait_send()
+        for d in [0] + near_order:
+            cot_x(d).wait_send()
+        cot_core().wait_send()
+        for i in fars:
+            far_copy(i).wait_send()
+        for i in range(len(spans)):
+            rest_core(i).wait_send()
+        part_copy().wait_send()
 
     for copy in sig_halo + cot_halo:
         copy.wait_send()
@@ -501,6 +586,44 @@
     wg_copies[1].wait()
 
 
+def finish(conv, sgrad, wgrad):
+    parts = 4
+
+    def body(conv_in, sg_in, wg_in, conv_out, sg_out, wg_out, held, wide, fields, sems):
+        ends = [(conv_in, fields.at[0], conv_out), (sg_in, fields.at[1], sg_out)]
+        ends += [(wg_in.at[k], held.at[k], wg_out.at[k]) for k in range(parts)]
+        loads = [pltpu.make_async_copy(a, b, sems.at[0, i]) for i, (a, b, _) in enumerate(ends)]
+        stores = [
+            pltpu.make_async_copy(b if i < 2 else wide.at[i - 2], c, sems.at[1, i])
+            for i, (_, b, c) in enumerate(ends)
+        ]
+        for copy in loads:
+            copy.start()
+        for i in range(2 + parts):
+            loads[i].wait()
+            if i >= 2:
+                wide[i - 2] = held[i - 2].astype(F32)
+            stores[i].start()
+        for copy in stores:
+            copy.wait()
+
+    return pl.pallas_call(
+        body,
+        out_shape=(
+            jax.ShapeDtypeStruct(conv.shape, conv.dtype),
+            jax.ShapeDtypeStruct(sgrad.shape, sgrad.dtype),
+            jax.ShapeDtypeStruct(wgrad.shape, F32),
+        ),
+        in_specs=[pl.BlockSpec(memory_space=pl.ANY)] * 3,
+        out_specs=[pl.BlockSpec(memory_space=pl.ANY)] * 3,
+        scratch_shapes=[
+            pltpu.VMEM(wgrad.shape, BF16), pltpu.VMEM(wgrad.shape, F32),
+            pltpu.VMEM((2,) + conv.shape, BF16), pltpu.SemaphoreType.DMA((2, 2 + parts)),
+        ],
+        compiler_params=pltpu.CompilerParams(vmem_limit_bytes=60 * 2**20),
+    )(conv, sgrad, wgrad)
+
+
 def local(signal, cotangent, weights, band_kernel, cycle_kernel, support_width):
     rows, _, chans = signal.shape
     nlat, nlon = lax.axis_size("lat"), lax.axis_size("lon")
@@ -510,7 +633,7 @@
     blocks, cells = rows // 8, rows * L
     half_rows = K * chans // 2
     piece = half_rows // nq
-    band = band_kernel.transpose(2, 0, 1, 3)
+    band = band_kernel.transpose(2, 3, 0, 1)
     cycle = cycle_kernel.transpose(0, 2, 1, 3)
     dma = pltpu.SemaphoreType.DMA
     ext = (rows + 2, L, chans)
@@ -520,26 +643,31 @@
     scratch = (
         [pltpu.VMEM(ext, BF16)] * 6
         + [pltpu.VMEM(weights.shape, BF16)]
-        + [pltpu.VMEM((2 * R + 1, K, rows + 32, 2 * H + 1), BF16)]
+        + [pltpu.VMEM(band.shape, BF16)]
         + [pltpu.VMEM((K, 2 * R + 1, 2 * P_SIZE, circle), BF16)]
         + [pltpu.SMEM(support_width.shape, jnp.int32)]
+        + [pltpu.VMEM((256, rows * nlat), F32), pltpu.VMEM((rows * nlat + 32, 256), BF16)]
         + [base] * 2 + [turns] * 2 + [matrices] * 2
         + [pltpu.VMEM((K, cells, chans), BF16), pltpu.VMEM((K, cells, chans), F32)]
         + [pltpu.VMEM((cells, chans), BF16)]
         + [pltpu.VMEM((rows, L, chans), BF16)] * 2
         + [pltpu.VMEM((SLAB + P_SIZE, X_HI, zn, 2, L, chans), BF16)]
-        + [pltpu.VMEM((K * P_SIZE * L, SLAB * circle), BF16)]
-        + [pltpu.VMEM((K * SLAB * L, P_SIZE * circle), BF16)]
-        + [pltpu.VMEM((K * SLAB * L, chans), F32)]
+        + [pltpu.VMEM((2, K * P_SIZE * L, SLAB * circle // 2), BF16)]
+        + [pltpu.VMEM((2, K * SLAB * L, P_SIZE * circle // 2), BF16)]
+        + [pltpu.VMEM((P_SIZE, K * SLAB * L, circle), BF16)]
+        + [pltpu.VMEM((K, zn // 2 * SLAB * L, chans), F32), pltpu.VMEM((zn // 2 * SLAB * L, chans), F32)]
+        + [pltpu.VMEM((K * (P_SIZE + SLAB) * L, chans), BF16)] * 2
+        + [pltpu.VMEM((K * (P_SIZE + SLAB) * L, chans), F32)]
         + [pltpu.VMEM((2 * half_rows, chans), F32)]
         + [pltpu.VMEM((half_rows, chans), BF16)] * 2
         + [pltpu.VMEM((nq, piece, chans), F32)]
         + [pltpu.VMEM((nq, piece, chans), BF16)] * 2
         + [pltpu.VMEM((n, piece // 2, 128), BF16) for n in (4, zn, 4)]
         + [pltpu.VMEM((2, nq, piece, chans), BF16)]
+        + [pltpu.SemaphoreType.REGULAR((2,))]
         + [dma((n,)) for n in (
-            8, 16, 16, 2, zn, zn, zn, zn, 2, 2,
-            zn, zn, 4,
+            6, 16, 16, 2, zn, zn, zn, zn, 2,
+            zn + 2, zn + 2, 3, 3, 2,
             2, nq, nq, zn, zn, 3, 3, nq, nq, 2, 4,
         )]
     )
@@ -551,11 +679,11 @@
         out_specs=[pl.BlockSpec(memory_space=pl.ANY)] * 3,
         scratch_shapes=scratch,
         compiler_params=pltpu.CompilerParams(
-            collective_id=0, has_side_effects=True, vmem_limit_bytes=40 * 2**20
+            collective_id=0, has_side_effects=True, vmem_limit_bytes=60 * 2**20
         ),
         cost_estimate=pl.CostEstimate(flops=10**9, bytes_accessed=4 * 10**6, transcendentals=0),
     )(signal, cotangent, weights, band, cycle, support_width)
-    return conv, sgrad, wgrad.astype(F32).reshape(K, chans, chans)
+    return finish(conv, sgrad, wgrad.reshape(K, chans, chans))
 
 
 def solution(mesh):

time: 65.7 us -> 61 us (0.928)
  local copies, waits for them, and re-layouts: 2.98 us -> 0 us
  other arithmetic: 1.06 us -> 0 us
    unnamed x13 -> x0, local copies, waits for them, and re-layouts: 2.98 us -> none
    pallas_call x1, Pallas kernels: 60.8 us -> 58.1 us  [local(): pl.pallas_call(kernel, out_shape=(field, field, jax.ShapeDtypeStruct((2,...]
    pallas_call x0 -> x1, Pallas kernels: none -> 2.18 us  [finish(): pl.pallas_call(body, out_shape=(jax.ShapeDtypeStruct(conv.shape, conv.dty...]
    reshape x1 -> x0, other arithmetic: 1.06 us -> none  [local(): return (conv, sgrad, wgrad.astype(F32).reshape(K, chans, chans))]
where the time goes in v3:
time: 61 us; the launch traced here: 60.9 us
  Pallas kernels  60.3 us (99%)
  between operations  0.64 us (1%)
    pallas_call x1, Pallas kernels, local(): pl.pallas_call(kernel, out_shape=(field, field, jax.ShapeDtypeStruct((2,...  58.1 us
    pallas_call x1, Pallas kernels, finish(): pl.pallas_call(body, out_shape=(jax.ShapeDtypeStruct(conv.shape, conv.dty...  2.18 us

profile of v3, /device:TPU:1, one launch (start us, length us, event | category | flops | bytes accessed | tf_op | source)
XLA Modules:
  0.0 60.9 jit_solution(17060617231570426441)
XLA Ops:
  0.6 58.1 %shard_map.85 = (bf16[48,8,256]{2,1,0:T(8,128)(2,1)}, bf16[48,8,256]{2,1,0:T(8,128)(2,1)}, bf16[2,16,32,256]{3,2,1,0:T(8,128)(2,1)}) custom-call(bf16[48,8,256]{2,1,0:T(8,128)(2,1)} %sig.1, bf16[48,8,256]{2,1,0:T(8,128)(2,1)} %cot.1, bf16[4,256,256]{2,1,0:T(8,128)(2,1)} %w_hbm.1, bf16[3,17,4,384]{3,2,1,0:T(4,128)(2,1)} %bitcast.4, ...), custom_call_target="tpu_custom_call" | custom-call | flops 1000000000 | bytes 4000000 | tf_op jit(solution)/shard_map/pallas_call | solution.py:675
  58.7 2.2 %shard_map.86 = (bf16[48,8,256]{2,1,0:T(8,128)(2,1)}, bf16[48,8,256]{2,1,0:T(8,128)(2,1)}, f32[4,256,256]{2,1,0:T(8,128)}) custom-call(bf16[48,8,256]{2,1,0:T(8,128)(2,1)} %get-tuple-element.6.conv_in, bf16[48,8,256]{2,1,0:T(8,128)(2,1)} %get-tuple-element.7.sg_in, bf16[4,256,256]{2,1,0:T(8,128)(2,1)} %bitcast.3), custom_call_target="tpu_custom_call" | custom-call | tf_op jit(solution)/shard_map/pallas_call | solution.py:610

commit v4 on v3

--- a/solution.py
+++ b/solution.py
@@ -35,7 +35,7 @@
     wall, wsend, wrecv, half, xs, xr, zs, zr, za, fin,
     far_sem, load_sem, halo_ss, halo_rs, own_sem, pc_ss, pc_rs, px_ss, px_rs, pk_sem,
     ps_ss, ps_rs, pb_ss, pb_rs, pp_sem,
-    core_sem, x_ss, x_rs, z_ss, z_rs, za_ss, za_rs, xa_ss, xa_rs, fc_sem, out_sem,
+    core_sem, x_ss, x_rs, z_ss, z_rs, za_ss, za_rs, xa_ss, xa_rs, fc_ss, fc_rs, out_sem,
 ):
     rows, _, chans = sig.shape
     nlat, nlon = lax.axis_size("lat"), lax.axis_size("lon")
@@ -99,13 +99,13 @@
     def greet(dev):
         pl.semaphore_signal(barrier, inc=1, device_id=dev, device_id_type=MESH)
 
+    @pl.when(is_polar)
+    def _():
+        for d in near_order:
+            greet(place((x + X_LO) % XS, y, (z + d) % zn, core))
+
     for d in near_order:
         greet(z_peer(d)[1])
-    @pl.when(is_polar)
-    def _():
-        for d in near_order:
-            greet(place((x + X_LO) % XS, y, (z + d) % zn, core))
-
     for o in xy_order:
         greet(xy_peer(o)[1])
     for dlat, dlon in ((1, 1), (1, -1), (-1, 1), (-1, -1), (0, 1), (0, -1)):
@@ -124,11 +124,6 @@
     ]
     for copy in loads:
         copy.start()
-    greeted = 6 + (nq - 1) + 2 * near
-    pl.semaphore_wait(barrier, jnp.where(is_polar, greeted + 2 * near, greeted))
-    for i, d in enumerate((near, zn - near)):
-        pl.semaphore_signal(far_sem.at[i], inc=1, device_id=z_peer(d)[1], device_id_type=MESH)
-
     slab_at = jnp.where(is_top, 0, rows - SLAB)
     pole_at = jnp.where(is_top, 0, rows - P_SIZE)
     sig_slab = sig.at[pl.ds(slab_at, SLAB)]
@@ -138,18 +133,16 @@
     def seen(d):
         return mid - d if d <= mid else mid + zn - d
 
-    def cot_z(d):
-        dst = slab.at[cot_rows, x_hi, seen(d), core]
-        return remote(cot_slab, dst, pc_ss.at[d], pc_rs.at[d], z_peer(d)[1])
-
-    def sig_z(d):
-        dst = slab.at[sig_rows, x_hi, seen(d), core]
-        return remote(sig_slab, dst, ps_ss.at[d], ps_rs.at[d], z_peer(d)[1])
+    def near_z(d):
+        src = slab.at[:, x_hi, mid, core]
+        dst = slab.at[:, x_hi, seen(d), core]
+        return remote(src, dst, pc_ss.at[d], pc_rs.at[d], z_peer(d)[1])
 
     def cot_x(d):
         dst = slab.at[cot_rows, x_hi, seen(d), core]
         dev = place((x + X_LO) % XS, y, (z + d) % zn, core)
-        return remote(cot_slab, dst, px_ss.at[d], px_rs.at[d], dev)
+        src = slab.at[cot_rows, x_hi, mid, core]
+        return remote(src, dst, px_ss.at[d], px_rs.at[d], dev)
 
     def cot_core():
         part = slab.at[cot_rows, :, pl.ds(mid - near, 2 * near + 1), core]
@@ -161,7 +154,7 @@
         )[i]
         return remote(
             slab.at[:, x_hi, pl.ds(src, n), core], slab.at[:, x_hi, pl.ds(dst, n), core],
-            ps_ss.at[zn + i], ps_rs.at[zn + i], z_peer(d)[1],
+            ps_ss.at[i], ps_rs.at[i], z_peer(d)[1],
         )
 
     fars = [0, 1] if near > 1 else [0]
@@ -183,15 +176,22 @@
 
     @pl.when(is_polar)
     def _():
-        own_slab[0].start()
-        own_slab[1].start()
+        for copy in own_slab:
+            copy.start()
+        for copy in own_slab:
+            copy.wait()
+
+    greeted = 6 + (nq - 1) + 2 * near
+    pl.semaphore_wait(barrier, jnp.where(is_polar, greeted + 2 * near, greeted))
+    for i, d in enumerate((near, zn - near)):
+        pl.semaphore_signal(far_sem.at[i], inc=1, device_id=z_peer(d)[1], device_id_type=MESH)
+
+    @pl.when(is_polar)
+    def _():
         for d in near_order:
             cot_x(d).start()
-        for d in near_order:
-            cot_z(d).start()
+            near_z(d).start()
         cot_x(0).start()
-        for d in near_order:
-            sig_z(d).start()
 
     def halo_copies(src, own, left, right, n):
         last, first = src.at[pl.ds(rows - 1, 1)], src.at[pl.ds(0, 1)]
@@ -213,7 +213,7 @@
 
     sig_halo = halo_copies(sig, s_o, s_l, s_r, 0)
     cot_halo = halo_copies(cot, c_o, c_l, c_r, 8)
-    for copy in sig_halo + cot_halo:
+    for copy in sig_halo:
         copy.start()
 
     loads[0].wait()
@@ -317,16 +317,22 @@
         for p in range(P_SIZE):
             turned = [cycle_rows(cyc, n * P_SIZE + p) for n in range(K * SLAB)]
             qt[p] = dot(jnp.concatenate(turned, 0).astype(BF16), pick).astype(BF16)
-        own_slab[0].wait()
-        for d in near_order:
-            cot_z(d).wait_recv()
         for d in [0] + near_order:
             cot_x(d).wait_recv()
+        for d in near_order:
+            near_z(d).wait_recv()
         cot_core().start()
 
     loads[3].wait()
     for copy in sig_halo:
         copy.wait_recv()
+    for copy in cot_halo:
+        copy.start()
+
+    @pl.when(is_polar)
+    def _():
+        for i in fars:
+            far_copy(i).start()
 
     def forward(b):
         part = dot(amat[b], window(s_o, s_l, s_r, b)).astype(BF16)
@@ -343,20 +349,12 @@
 
     loop(0, blocks, fold)
 
-    for k in range(K):
-        wall[pl.ds(k * chans, chans), :] = lax.dot_general(
-            filt[k], cot2[...], (((0,), (0,)), ((), ())), preferred_element_type=F32
-        )
-
     def cells(ref):
         held = ref.astype(F32)
         return held.reshape(-1, chans)
 
     @pl.when(is_polar)
     def _():
-        own_slab[1].wait()
-        for d in near_order:
-            sig_z(d).wait_recv()
         cot_core().wait_recv()
         for i in range(2 * near):
             t = i - near
@@ -370,20 +368,31 @@
             for k in range(K):
                 gw[k, pl.ds(i * SLAB * L, SLAB * L), :] = turned[k * SLAB * L : (k + 1) * SLAB * L]
             sw[pl.ds(i * SLAB * L, SLAB * L), :] = cells(slab[0:SLAB, x_hi, mid - t, core])
-        for k in range(K):
-            wall[pl.ds(k * chans, chans), :] += lax.dot_general(
-                sw[...].astype(BF16), gw[k].astype(BF16),
-                (((0,), (0,)), ((), ())), preferred_element_type=F32,
+    half_rows = K * chans // 2
+
+    def weight_half(c):
+        for i in range(K // 2):
+            k = c * (K // 2) + i
+            wall[pl.ds(i * chans, chans), :] = lax.dot_general(
+                filt[k], cot2[...], (((0,), (0,)), ((), ())), preferred_element_type=F32
             )
 
-    half_rows = K * chans // 2
-    wsend[...] = wall[pl.ds(pl.multiple_of((1 - core) * half_rows, 8), half_rows), :].astype(BF16)
+        @pl.when(is_polar)
+        def _():
+            for i in range(K // 2):
+                wall[pl.ds(i * chans, chans), :] += lax.dot_general(
+                    sw[...].astype(BF16), gw[c * (K // 2) + i].astype(BF16),
+                    (((0,), (0,)), ((), ())), preferred_element_type=F32,
+                )
+
+    weight_half(1 - core)
+    wsend[...] = wall[...].astype(BF16)
     to_core = remote(wsend, wrecv, core_sem.at[0], core_sem.at[1], partner)
     to_core.start()
+    weight_half(core)
     piece = half_rows // nq
-    mine = wall[pl.ds(pl.multiple_of(core * half_rows, 8), half_rows), :]
     to_core.wait_recv()
-    summed = mine + wrecv[...].astype(F32)
+    summed = wall[...] + wrecv[...].astype(F32)
     half[...] = summed.reshape(nq, piece, chans)
     xs[...] = summed.astype(BF16).reshape(nq, piece, chans)
 
@@ -393,11 +402,6 @@
 
     for o in xy_order:
         xy_copy(o).start()
-
-    @pl.when(is_polar)
-    def _():
-        for i in fars:
-            far_copy(i).start()
 
     for i in range(2):
         pl.semaphore_wait(far_sem.at[i], 1)
@@ -412,7 +416,6 @@
 
     loop(0, rows // chunk, mix_out)
     build(bb, bmat, True)
-
     for copy in cot_halo:
         copy.wait_recv()
 
@@ -423,6 +426,30 @@
 
     loop(0, blocks, backward)
 
+    @pl.when(is_polar)
+    def _():
+        start = cyc[...]
+        from_lag = lax.broadcasted_iota(jnp.int32, (circle, circle), 0)
+        to_lag = lax.broadcasted_iota(jnp.int32, (circle, circle), 1)
+        turned = ((from_lag + to_lag) % circle == 0).astype(F32).astype(BF16)
+        rev[...] = pltpu.roll(dot(start.astype(BF16), turned), lon * L, 1)
+        cyc[...] = pltpu.roll(start, lon * L, 1)
+        side = circle // 2
+        shift = (side + (mid - z) * 2 * L) % side
+
+        def circulant(src, rows_of, dst, at):
+            full = jnp.concatenate([cycle_rows(src, n) for n in rows_of], 0)
+            for h in range(2):
+                turned_side = pltpu.roll(full[:, h * side : (h + 1) * side], shift, 1)
+                dst[h, :, pl.ds(at, side)] = turned_side.astype(BF16)
+
+        for p in range(P_SIZE):
+            circulant(cyc, [n * P_SIZE + p for n in range(K * SLAB)], qb, p * side)
+        for r in taps:
+            circulant(
+                rev, [(k * SLAB + r) * P_SIZE + p for k in range(K) for p in range(P_SIZE)], qf, r * side
+            )
+
     loop(1, nq, lambda o: xy_copy(o).wait_recv())
     total = half[me_q]
     for o in range(1, nq):
@@ -446,6 +473,50 @@
             far_copy(i).wait_recv()
         for i in range(len(spans)):
             rest_core(i).start()
+
+    @pl.when(is_polar)
+    def _():
+        for i in range(len(spans)):
+            rest_core(i).wait_recv()
+        side = circle // 2
+        held_rows = [cells(slab[r, x_hi]).astype(BF16) for r in range(SLAB + P_SIZE)]
+
+        def share(h):
+            front = sum(dot(qf[h, :, r * side : (r + 1) * side], held_rows[r]) for r in range(SLAB))
+            back = sum(
+                dot(qb[h, :, p * side : (p + 1) * side], held_rows[SLAB + p]) for p in range(P_SIZE)
+            )
+            return jnp.concatenate([front, back], 0)
+
+        part_s[...] = share(1 - x_hi).astype(BF16)
+        part_copy().start()
+        own_part[...] = share(x_hi)
+
+    loop(0, zn - 1, lambda i: z_copy(z_offset(i)).wait_recv())
+    acc = zr[0].astype(F32)
+    for s in range(1, zn):
+        acc = acc + zr[s].astype(F32)
+    za[z % 4] = (acc * F32(1.0 / math.sqrt(total_rows * circle))).astype(BF16)
+    hand = (2, 1, zn - 1)
+
+    def za_copy(i):
+        dst = za.at[z % 4]
+        return remote(dst, dst, za_ss.at[i], za_rs.at[i], z_peer(hand[i])[1])
+
+    for i in range(3):
+        za_copy(i).start()
+
+    for i in range(3):
+        za_copy(i).wait_recv()
+    lines = [jnp.concatenate([za[2 * i].astype(F32), za[2 * i + 1].astype(F32)], 1) for i in range(2)]
+    fin[core, me_q] = jnp.concatenate(lines, 0).astype(BF16)
+
+    def xa_copy(o):
+        dst = fin.at[core, me_q]
+        return remote(dst, dst, xa_ss.at[o], xa_rs.at[o], xy_peer(o)[1])
+
+    for o in xy_order:
+        xa_copy(o).start()
 
     def mix_back(b):
         at = pl.ds(b * chunk * L, chunk * L)
@@ -459,71 +530,6 @@
         sg_v[pl.ds(b * chunk, chunk)] = acc.reshape(chunk, L, chans).astype(BF16)
 
     loop(0, rows // chunk, mix_back)
-
-    @pl.when(is_polar)
-    def _():
-        start = cyc[...]
-        from_lag = lax.broadcasted_iota(jnp.int32, (circle, circle), 0)
-        to_lag = lax.broadcasted_iota(jnp.int32, (circle, circle), 1)
-        turned = ((from_lag + to_lag) % circle == 0).astype(F32).astype(BF16)
-        rev[...] = pltpu.roll(dot(start.astype(BF16), turned), lon * L, 1)
-        cyc[...] = pltpu.roll(start, lon * L, 1)
-        side = circle // 2
-        shift = (side + (mid - z) * 2 * L) % side
-
-        def circulant(src, rows_of, dst, at):
-            full = jnp.concatenate([cycle_rows(src, n) for n in rows_of], 0)
-            for h in range(2):
-                turned_side = pltpu.roll(full[:, h * side : (h + 1) * side], shift, 1)
-                dst[h, :, pl.ds(at, side)] = turned_side.astype(BF16)
-
-        for p in range(P_SIZE):
-            circulant(cyc, [n * P_SIZE + p for n in range(K * SLAB)], qb, p * side)
-        for r in taps:
-            circulant(
-                rev, [(k * SLAB + r) * P_SIZE + p for k in range(K) for p in range(P_SIZE)], qf, r * side
-            )
-
-        for i in range(len(spans)):
-            rest_core(i).wait_recv()
-        held_rows = [cells(slab[r, x_hi]).astype(BF16) for r in range(SLAB + P_SIZE)]
-
-        def share(h):
-            front = sum(dot(qf[h, :, r * side : (r + 1) * side], held_rows[r]) for r in range(SLAB))
-            back = sum(
-                dot(qb[h, :, p * side : (p + 1) * side], held_rows[SLAB + p]) for p in range(P_SIZE)
-            )
-            return jnp.concatenate([front, back], 0)
-
-        part_s[...] = share(1 - x_hi).astype(BF16)
-        part_copy().start()
-        own_part[...] = share(x_hi)
-
-    loop(0, zn - 1, lambda i: z_copy(z_offset(i)).wait_recv())
-    acc = zr[0].astype(F32)
-    for s in range(1, zn):
-        acc = acc + zr[s].astype(F32)
-    za[z % 4] = (acc * F32(1.0 / math.sqrt(total_rows * circle))).astype(BF16)
-    hand = (2, 1, zn - 1)
-
-    def za_copy(i):
-        dst = za.at[z % 4]
-        return remote(dst, dst, za_ss.at[i], za_rs.at[i], z_peer(hand[i])[1])
-
-    for i in range(3):
-        za_copy(i).start()
-
-    for i in range(3):
-        za_copy(i).wait_recv()
-    lines = [jnp.concatenate([za[2 * i].astype(F32), za[2 * i + 1].astype(F32)], 1) for i in range(2)]
-    fin[core, me_q] = jnp.concatenate(lines, 0).astype(BF16)
-
-    def xa_copy(o):
-        dst = fin.at[core, me_q]
-        return remote(dst, dst, xa_ss.at[o], xa_rs.at[o], xy_peer(o)[1])
-
-    for o in xy_order:
-        xa_copy(o).start()
 
     @pl.when(is_polar)
     def _():
@@ -547,20 +553,29 @@
     conv_copy = pltpu.make_async_copy(conv_v, conv_out, out_sem.at[0])
     conv_copy.start()
 
-    loop(1, nq, lambda o: xa_copy(o).wait_recv())
-    swap = remote(fin.at[core], fin.at[core], fc_sem.at[0], fc_sem.at[1], partner)
-    swap.start()
-    wg_copies = [
-        pltpu.make_async_copy(fin.at[c], wgrad_out.at[c], out_sem.at[2 + i])
-        for i, c in enumerate((core, 1 - core))
-    ]
-    wg_copies[0].start()
+    def column(c, dx):
+        return fin.at[c, pl.ds((x - dx + XS) % XS * ys, ys)]
+
+    def swap(i, dx):
+        part = column(core, dx)
+        return remote(part, part, fc_ss.at[i], fc_rs.at[i], partner)
+
+    def leave(i, c, dx):
+        dst = wgrad_out.at[c, pl.ds((x - dx + XS) % XS * ys, ys)]
+        return pltpu.make_async_copy(column(c, dx), dst, out_sem.at[i])
+
+    columns = list(enumerate((0, 1, XS - 1, 2)))
+    for i, dx in columns:
+        for o in range(dx * ys, (dx + 1) * ys):
+            if o > 0:
+                xa_copy(o).wait_recv()
+        swap(i, dx).start()
+        leave(2 + i, core, dx).start()
 
     @pl.when(is_polar)
     def _():
         for d in near_order:
-            cot_z(d).wait_send()
-            sig_z(d).wait_send()
+            near_z(d).wait_send()
         for d in [0] + near_order:
             cot_x(d).wait_send()
         cot_core().wait_send()
@@ -580,10 +595,12 @@
     loop(1, nq, lambda o: xa_copy(o).wait_send())
     conv_copy.wait()
     sg_copy.wait()
-    swap.wait()
-    wg_copies[1].start()
-    wg_copies[0].wait()
-    wg_copies[1].wait()
+    for i, dx in columns:
+        swap(i, dx).wait()
+        leave(2 + XS + i, 1 - core, dx).start()
+    for i, dx in columns:
+        leave(2 + i, core, dx).wait()
+        leave(2 + XS + i, 1 - core, dx).wait()
 
 
 def finish(conv, sgrad, wgrad):
@@ -658,7 +675,7 @@
         + [pltpu.VMEM((K, zn // 2 * SLAB * L, chans), F32), pltpu.VMEM((zn // 2 * SLAB * L, chans), F32)]
         + [pltpu.VMEM((K * (P_SIZE + SLAB) * L, chans), BF16)] * 2
         + [pltpu.VMEM((K * (P_SIZE + SLAB) * L, chans), F32)]
-        + [pltpu.VMEM((2 * half_rows, chans), F32)]
+        + [pltpu.VMEM((half_rows, chans), F32)]
         + [pltpu.VMEM((half_rows, chans), BF16)] * 2
         + [pltpu.VMEM((nq, piece, chans), F32)]
         + [pltpu.VMEM((nq, piece, chans), BF16)] * 2
@@ -667,8 +684,8 @@
         + [pltpu.SemaphoreType.REGULAR((2,))]
         + [dma((n,)) for n in (
             6, 16, 16, 2, zn, zn, zn, zn, 2,
-            zn + 2, zn + 2, 3, 3, 2,
-            2, nq, nq, zn, zn, 3, 3, nq, nq, 2, 4,
+            2, 2, 3, 3, 2,
+            2, nq, nq, zn, zn, 3, 3, nq, nq, XS, XS, 2 + 2 * XS,
         )]
     )
     field = jax.ShapeDtypeStruct(signal.shape, BF16)

time: 61 us -> 59.1 us (0.969)
  Pallas kernels: 60.3 us -> 58.3 us
    pallas_call x1, Pallas kernels: 58.1 us -> 56.1 us  [local(): pl.pallas_call(kernel, out_shape=(field, field, jax.ShapeDtypeStruct((2,...]
where the time goes in v4:
time: 59.1 us; the launch traced here: 58.9 us
  Pallas kernels  58.3 us (99%)
  between operations  0.64 us (1%)
    pallas_call x1, Pallas kernels, local(): pl.pallas_call(kernel, out_shape=(field, field, jax.ShapeDtypeStruct((2,...  56.1 us
    pallas_call x1, Pallas kernels, finish(): pl.pallas_call(body, out_shape=(jax.ShapeDtypeStruct(conv.shape, conv.dty...  2.18 us

profile of v4, /device:TPU:1, one launch (start us, length us, event | category | flops | bytes accessed | tf_op | source)
XLA Modules:
  0.0 58.9 jit_solution(12482079762893501634)
XLA Ops:
  0.6 56.1 %shard_map.85 = (bf16[48,8,256]{2,1,0:T(8,128)(2,1)}, bf16[48,8,256]{2,1,0:T(8,128)(2,1)}, bf16[2,16,32,256]{3,2,1,0:T(8,128)(2,1)}) custom-call(bf16[48,8,256]{2,1,0:T(8,128)(2,1)} %sig.1, bf16[48,8,256]{2,1,0:T(8,128)(2,1)} %cot.1, bf16[4,256,256]{2,1,0:T(8,128)(2,1)} %w_hbm.1, bf16[3,17,4,384]{3,2,1,0:T(4,128)(2,1)} %bitcast.4, ...), custom_call_target="tpu_custom_call" | custom-call | flops 1000000000 | bytes 4000000 | tf_op jit(solution)/shard_map/pallas_call | solution.py:692
  56.8 2.2 %shard_map.86 = (bf16[48,8,256]{2,1,0:T(8,128)(2,1)}, bf16[48,8,256]{2,1,0:T(8,128)(2,1)}, f32[4,256,256]{2,1,0:T(8,128)}) custom-call(bf16[48,8,256]{2,1,0:T(8,128)(2,1)} %get-tuple-element.6.conv_in, bf16[48,8,256]{2,1,0:T(8,128)(2,1)} %get-tuple-element.7.sg_in, bf16[4,256,256]{2,1,0:T(8,128)(2,1)} %bitcast.3), custom_call_target="tpu_custom_call" | custom-call | tf_op jit(solution)/shard_map/pallas_call | solution.py:627

commit v5 on v4

--- a/solution.py
+++ b/solution.py
@@ -326,9 +326,6 @@
     loads[3].wait()
     for copy in sig_halo:
         copy.wait_recv()
-    for copy in cot_halo:
-        copy.start()
-
     @pl.when(is_polar)
     def _():
         for i in fars:
@@ -402,6 +399,8 @@
 
     for o in xy_order:
         xy_copy(o).start()
+    for copy in cot_halo:
+        copy.start()
 
     for i in range(2):
         pl.semaphore_wait(far_sem.at[i], 1)
@@ -416,16 +415,6 @@
 
     loop(0, rows // chunk, mix_out)
     build(bb, bmat, True)
-    for copy in cot_halo:
-        copy.wait_recv()
-
-    def backward(b):
-        part = dot(bmat[b], window(c_o, c_l, c_r, b))
-        for k in range(K):
-            grad[k, pl.ds(b * 64, 64), :] = part[k * 64 : (k + 1) * 64]
-
-    loop(0, blocks, backward)
-
     @pl.when(is_polar)
     def _():
         start = cyc[...]
@@ -491,6 +480,16 @@
         part_s[...] = share(1 - x_hi).astype(BF16)
         part_copy().start()
         own_part[...] = share(x_hi)
+
+    for copy in cot_halo:
+        copy.wait_recv()
+
+    def backward(b):
+        part = dot(bmat[b], window(c_o, c_l, c_r, b))
+        for k in range(K):
+            grad[k, pl.ds(b * 64, 64), :] = part[k * 64 : (k + 1) * 64]
+
+    loop(0, blocks, backward)
 
     loop(0, zn - 1, lambda i: z_copy(z_offset(i)).wait_recv())
     acc = zr[0].astype(F32)

time: 59.1 us -> 58.4 us (0.988)
  Pallas kernels: 58.3 us -> 57.6 us
    pallas_call x1, Pallas kernels: 56.1 us -> 55.4 us  [local(): pl.pallas_call(kernel, out_shape=(field, field, jax.ShapeDtypeStruct((2,...]
where the time goes in v5:
time: 58.4 us; the launch traced here: 58.3 us
  Pallas kernels  57.6 us (99%)
  between operations  0.64 us (1%)
    pallas_call x1, Pallas kernels, local(): pl.pallas_call(kernel, out_shape=(field, field, jax.ShapeDtypeStruct((2,...  55.4 us
    pallas_call x1, Pallas kernels, finish(): pl.pallas_call(body, out_shape=(jax.ShapeDtypeStruct(conv.shape, conv.dty...  2.18 us

profile of v5, /device:TPU:1, one launch (start us, length us, event | category | flops | bytes accessed | tf_op | source)
XLA Modules:
  0.0 58.3 jit_solution(8734250342112150878)
XLA Ops:
  0.6 55.4 %shard_map.85 = (bf16[48,8,256]{2,1,0:T(8,128)(2,1)}, bf16[48,8,256]{2,1,0:T(8,128)(2,1)}, bf16[2,16,32,256]{3,2,1,0:T(8,128)(2,1)}) custom-call(bf16[48,8,256]{2,1,0:T(8,128)(2,1)} %sig.1, bf16[48,8,256]{2,1,0:T(8,128)(2,1)} %cot.1, bf16[4,256,256]{2,1,0:T(8,128)(2,1)} %w_hbm.1, bf16[3,17,4,384]{3,2,1,0:T(4,128)(2,1)} %bitcast.4, ...), custom_call_target="tpu_custom_call" | custom-call | flops 1000000000 | bytes 4000000 | tf_op jit(solution)/shard_map/pallas_call | solution.py:691
  56.1 2.2 %shard_map.86 = (bf16[48,8,256]{2,1,0:T(8,128)(2,1)}, bf16[48,8,256]{2,1,0:T(8,128)(2,1)}, f32[4,256,256]{2,1,0:T(8,128)}) custom-call(bf16[48,8,256]{2,1,0:T(8,128)(2,1)} %get-tuple-element.6.conv_in, bf16[48,8,256]{2,1,0:T(8,128)(2,1)} %get-tuple-element.7.sg_in, bf16[4,256,256]{2,1,0:T(8,128)(2,1)} %bitcast.3), custom_call_target="tpu_custom_call" | custom-call | tf_op jit(solution)/shard_map/pallas_call | solution.py:626

commit v6 on v5

--- a/solution.py
+++ b/solution.py
@@ -122,8 +122,6 @@
             (w_hbm, w),
         ))
     ]
-    for copy in loads:
-        copy.start()
     slab_at = jnp.where(is_top, 0, rows - SLAB)
     pole_at = jnp.where(is_top, 0, rows - P_SIZE)
     sig_slab = sig.at[pl.ds(slab_at, SLAB)]
@@ -178,6 +176,12 @@
     def _():
         for copy in own_slab:
             copy.start()
+
+    for copy in loads[:4]:
+        copy.start()
+
+    @pl.when(is_polar)
+    def _():
         for copy in own_slab:
             copy.wait()
 
@@ -214,6 +218,8 @@
     sig_halo = halo_copies(sig, s_o, s_l, s_r, 0)
     cot_halo = halo_copies(cot, c_o, c_l, c_r, 8)
     for copy in sig_halo:
+        copy.start()
+    for copy in loads[4:]:
         copy.start()
 
     loads[0].wait()
@@ -367,28 +373,34 @@
             sw[pl.ds(i * SLAB * L, SLAB * L), :] = cells(slab[0:SLAB, x_hi, mid - t, core])
     half_rows = K * chans // 2
 
-    def weight_half(c):
-        for i in range(K // 2):
-            k = c * (K // 2) + i
-            wall[pl.ds(i * chans, chans), :] = lax.dot_general(
-                filt[k], cot2[...], (((0,), (0,)), ((), ())), preferred_element_type=F32
-            )
+    def weight_part(c, i):
+        k = c * (K // 2) + i
+        at = pl.ds(i * chans, chans)
+        wall[at, :] = lax.dot_general(
+            filt[k], cot2[...], (((0,), (0,)), ((), ())), preferred_element_type=F32
+        )
 
         @pl.when(is_polar)
         def _():
-            for i in range(K // 2):
-                wall[pl.ds(i * chans, chans), :] += lax.dot_general(
-                    sw[...].astype(BF16), gw[c * (K // 2) + i].astype(BF16),
-                    (((0,), (0,)), ((), ())), preferred_element_type=F32,
-                )
-
-    weight_half(1 - core)
-    wsend[...] = wall[...].astype(BF16)
-    to_core = remote(wsend, wrecv, core_sem.at[0], core_sem.at[1], partner)
-    to_core.start()
-    weight_half(core)
+            wall[at, :] += lax.dot_general(
+                sw[...].astype(BF16), gw[k].astype(BF16),
+                (((0,), (0,)), ((), ())), preferred_element_type=F32,
+            )
+
+    def to_core(i):
+        at = pl.ds(i * chans, chans)
+        return remote(wsend.at[at], wrecv.at[at], core_sem.at[i], core_sem.at[K // 2 + i], partner)
+
+    for i in range(K // 2):
+        weight_part(1 - core, i)
+        at = pl.ds(i * chans, chans)
+        wsend[at, :] = wall[at, :].astype(BF16)
+        to_core(i).start()
+    for i in range(K // 2):
+        weight_part(core, i)
     piece = half_rows // nq
-    to_core.wait_recv()
+    for i in range(K // 2):
+        to_core(i).wait_recv()
     summed = wall[...] + wrecv[...].astype(F32)
     half[...] = summed.reshape(nq, piece, chans)
     xs[...] = summed.astype(BF16).reshape(nq, piece, chans)
@@ -586,7 +598,8 @@
 
     for copy in sig_halo + cot_halo:
         copy.wait_send()
-    to_core.wait_send()
+    for i in range(K // 2):
+        to_core(i).wait_send()
     loop(1, nq, lambda o: xy_copy(o).wait_send())
     loop(1, zn, lambda d: z_copy(d).wait_send())
     for i in range(3):
@@ -684,7 +697,7 @@
         + [dma((n,)) for n in (
             6, 16, 16, 2, zn, zn, zn, zn, 2,
             2, 2, 3, 3, 2,
-            2, nq, nq, zn, zn, 3, 3, nq, nq, XS, XS, 2 + 2 * XS,
+            K, nq, nq, zn, zn, 3, 3, nq, nq, XS, XS, 2 + 2 * XS,
         )]
     )
     field = jax.ShapeDtypeStruct(signal.shape, BF16)

time: 58.4 us -> 59.9 us (1.026)
  Pallas kernels: 57.6 us -> 59.1 us
    pallas_call x1, Pallas kernels: 55.4 us -> 56.9 us  [local(): pl.pallas_call(kernel, out_shape=(field, field, jax.ShapeDtypeStruct((2,...]
where the time goes in v6:
time: 59.9 us; the launch traced here: 59.7 us
  Pallas kernels  59.1 us (99%)
  between operations  0.64 us (1%)
    pallas_call x1, Pallas kernels, local(): pl.pallas_call(kernel, out_shape=(field, field, jax.ShapeDtypeStruct((2,...  56.9 us
    pallas_call x1, Pallas kernels, finish(): pl.pallas_call(body, out_shape=(jax.ShapeDtypeStruct(conv.shape, conv.dty...  2.18 us

profile of v6, /device:TPU:1, one launch (start us, length us, event | category | flops | bytes accessed | tf_op | source)
XLA Modules:
  0.0 59.7 jit_solution(5990698304055026367)
XLA Ops:
  0.6 56.9 %shard_map.85 = (bf16[48,8,256]{2,1,0:T(8,128)(2,1)}, bf16[48,8,256]{2,1,0:T(8,128)(2,1)}, bf16[2,16,32,256]{3,2,1,0:T(8,128)(2,1)}) custom-call(bf16[48,8,256]{2,1,0:T(8,128)(2,1)} %sig.1, bf16[48,8,256]{2,1,0:T(8,128)(2,1)} %cot.1, bf16[4,256,256]{2,1,0:T(8,128)(2,1)} %w_hbm.1, bf16[3,17,4,384]{3,2,1,0:T(4,128)(2,1)} %bitcast.4, ...), custom_call_target="tpu_custom_call" | custom-call | flops 1000000000 | bytes 4000000 | tf_op jit(solution)/shard_map/pallas_call | solution.py:704
  57.5 2.2 %shard_map.86 = (bf16[48,8,256]{2,1,0:T(8,128)(2,1)}, bf16[48,8,256]{2,1,0:T(8,128)(2,1)}, f32[4,256,256]{2,1,0:T(8,128)}) custom-call(bf16[48,8,256]{2,1,0:T(8,128)(2,1)} %get-tuple-element.6.conv_in, bf16[48,8,256]{2,1,0:T(8,128)(2,1)} %get-tuple-element.7.sg_in, bf16[4,256,256]{2,1,0:T(8,128)(2,1)} %bitcast.3), custom_call_target="tpu_custom_call" | custom-call | tf_op jit(solution)/shard_map/pallas_call | solution.py:639
